TPU v7x, 256 devices: a whole 4x4x8 slice. The times are simulated.
256 devices in a mesh: dp: 8 (over z_hi, x), ctx: 32 (over y, z_lo, core).
Axes of the slice: x: 4, y: 4, z: 8 (z_hi: 2, z_lo: 4; z = z_hi * 4 + z_lo), core: 2. Of those that a mesh axis runs over, the one named last changes fastest.
Arguments:
- queries: bfloat16 [65536, 1792], P(('dp', 'ctx')), parts along dimension 0, may hold values from -8 to 8
- keys: bfloat16 [65536, 256], P(('dp', 'ctx')), parts along dimension 0, may hold values from -8 to 8
- values: bfloat16 [65536, 256], P(('dp', 'ctx')), parts along dimension 0, may hold values from -6 to 6
- output_gradient: bfloat16 [65536, 1792], P(('dp', 'ctx')), parts along dimension 0, may hold values from -6 to 6
- lengths: int32 [256], P('dp'), parts along dimension 0, may hold values from 1 to 768, 8192 in all
Outputs:
- attended: bfloat16 [65536, 1792], P(('dp', 'ctx')), parts along dimension 0
- grad_queries: bfloat16 [65536, 1792], P(('dp', 'ctx')), parts along dimension 0
- grad_keys: bfloat16 [65536, 256], P(('dp', 'ctx')), parts along dimension 0
- grad_values: bfloat16 [65536, 256], P(('dp', 'ctx')), parts along dimension 0
There are 8 independent parts, one for each index of `dp`. A program takes and returns all parts, laid end to end along the dimension named above; each array names one. Nothing has to cross between parts.
Inputs may be any that keep to these rules, and one draw needn't show every extreme that they name: The lengths of a row sum to 8192; the longest is exactly 768.
All inputs are finite; a program needn't handle non-finite values.
Results may differ from a plain program's by a relative error of at most 0.029.
Values may be sent and summed in bfloat16 or wider, within the bound.
A program may use at most 192 MiB of HBM per device.

v0:
```python
import math

import jax
import jax.numpy as jnp
from jax import lax
from jax.sharding import PartitionSpec as P

QUERY_HEADS = 14
KEY_VALUE_HEADS = 2
HEAD_SIZE = 128


NEGATIVE_FILL = -1e30


def shifted(value, axis, by):
    length = lax.axis_size(axis)
    pairs = [(i, i + by) for i in range(length) if 0 <= i + by < length]
    return lax.ppermute(value, axis, pairs)


def doc_ids(positions, lengths):
    ends = jnp.cumsum(lengths)
    return jnp.sum((positions[:, None] >= ends[None, :]).astype(jnp.int32), axis=1)


def tile_mask(q_pos, k_pos, q_doc, k_doc):
    inside = (
        (k_pos[None, :] <= q_pos[:, None])
        & (k_pos[None, :] >= 0)
        & (q_doc[:, None] == k_doc[None, :])
    )
    return inside[None, None]


def tile_scores(query_heads, k_tile, scale):
    return (
        jnp.einsum("rkgd,wkd->kgrw", query_heads, k_tile, preferred_element_type=jnp.float32)
        * scale
    )


def grad_terms(scores, heads_gradient, v_tile, mask, lse, delta, scale):
    probs = jnp.where(mask, jnp.exp(scores - lse), 0.0)
    lower_bound = probs.astype(jnp.bfloat16)
    dprob = jnp.einsum("rkgd,wkd->kgrw", heads_gradient, v_tile, preferred_element_type=jnp.float32)
    score_gradient = (probs * (dprob - delta) * scale).astype(jnp.bfloat16)
    return (lower_bound, score_gradient)


def per_device(queries, keys, values, output_gradient, lengths):
    count = lax.axis_size("ctx")
    here = lax.axis_index("ctx")
    row_batch = queries.shape[0]
    group_factor = QUERY_HEADS // KEY_VALUE_HEADS
    before = count // 8 - 1
    window_width = (before + 1) * row_batch
    tile = 2 * row_batch
    tiles = window_width // tile
    scale = 1.0 / math.sqrt(HEAD_SIZE)
    pair = jnp.stack([keys, values])
    parts = [shifted(pair, "ctx", dist) for dist in range(before, 0, -1)]
    parts.append(pair)
    window_span = jnp.concatenate(parts, axis=1)
    window_keys = window_span[0].reshape(window_width, KEY_VALUE_HEADS, HEAD_SIZE)
    window_values = window_span[1].reshape(window_width, KEY_VALUE_HEADS, HEAD_SIZE)
    q_pos = here * row_batch + jnp.arange(row_batch, dtype=jnp.int32)
    k_pos = here * row_batch - before * row_batch + jnp.arange(window_width, dtype=jnp.int32)
    q_doc = doc_ids(q_pos, lengths)
    k_doc = doc_ids(k_pos, lengths)
    query_heads = queries.reshape(row_batch, KEY_VALUE_HEADS, group_factor, HEAD_SIZE)
    heads_gradient = output_gradient.reshape(row_batch, KEY_VALUE_HEADS, group_factor, HEAD_SIZE)

    def process_tiles(work, carry):
        for index in range(tiles):
            carry = work(index, carry)
        return carry

    def stats_tile(index, carry):
        top, total, store = carry
        low_end = index * tile
        mask = tile_mask(
            q_pos, k_pos[low_end : low_end + tile], q_doc, k_doc[low_end : low_end + tile]
        )
        raw = tile_scores(query_heads, window_keys[low_end : low_end + tile], scale)
        store = store.at[..., low_end : low_end + tile].set(raw)
        scores = jnp.where(mask, raw, NEGATIVE_FILL)
        new_top = jnp.maximum(top, jnp.max(scores, axis=-1))
        total = total * jnp.exp(top - new_top) + jnp.sum(
            jnp.where(mask, jnp.exp(scores - new_top[..., None]), 0.0), axis=-1
        )
        return (new_top, total, store)

    blank_storage = jnp.zeros((KEY_VALUE_HEADS, group_factor, row_batch, window_width), jnp.float32)
    start_stats = (
        jnp.full((KEY_VALUE_HEADS, group_factor, row_batch), NEGATIVE_FILL, jnp.float32),
        jnp.zeros((KEY_VALUE_HEADS, group_factor, row_batch), jnp.float32),
        blank_storage,
    )
    top, total, store = process_tiles(stats_tile, start_stats)
    lse_rows = top + jnp.log(total)
    lse = lse_rows[..., None]

    def tile_raw(index):
        low_end = index * tile
        return store[..., low_end : low_end + tile]

    def output_tile(index, acc):
        low_end = index * tile
        mask = tile_mask(
            q_pos, k_pos[low_end : low_end + tile], q_doc, k_doc[low_end : low_end + tile]
        )
        scores = tile_raw(index)
        probs = jnp.where(mask, jnp.exp(scores - lse), 0.0).astype(jnp.bfloat16)
        return acc + jnp.einsum(
            "kgrw,wkd->rkgd",
            probs,
            window_values[low_end : low_end + tile],
            preferred_element_type=jnp.float32,
        )

    output_heads = process_tiles(
        output_tile, jnp.zeros((row_batch, KEY_VALUE_HEADS, group_factor, HEAD_SIZE), jnp.float32)
    ).astype(jnp.bfloat16)
    delta_rows = jnp.transpose(
        jnp.sum(heads_gradient.astype(jnp.float32) * output_heads.astype(jnp.float32), axis=-1),
        (1, 2, 0),
    )
    delta = delta_rows[..., None]

    def back_tile(index, carry):
        grad_q, key_window_gradient, value_window_gradient = carry
        low_end = index * tile
        k_tile = window_keys[low_end : low_end + tile]
        v_tile = window_values[low_end : low_end + tile]
        mask = tile_mask(
            q_pos, k_pos[low_end : low_end + tile], q_doc, k_doc[low_end : low_end + tile]
        )
        lower_bound, score_gradient = grad_terms(
            tile_raw(index), heads_gradient, v_tile, mask, lse, delta, scale
        )
        grad_q = grad_q + jnp.einsum(
            "kgrw,wkd->rkgd", score_gradient, k_tile, preferred_element_type=jnp.float32
        )
        key_window_gradient = key_window_gradient.at[low_end : low_end + tile].set(
            jnp.einsum(
                "cmsl,scme->lce", score_gradient, query_heads, preferred_element_type=jnp.float32
            )
        )
        value_window_gradient = value_window_gradient.at[low_end : low_end + tile].set(
            jnp.einsum(
                "cmsl,scme->lce", lower_bound, heads_gradient, preferred_element_type=jnp.float32
            )
        )
        return (grad_q, key_window_gradient, value_window_gradient)

    blank_window = jnp.zeros((window_width, KEY_VALUE_HEADS, HEAD_SIZE), jnp.float32)
    backward_start = (
        jnp.zeros((row_batch, KEY_VALUE_HEADS, group_factor, HEAD_SIZE), jnp.float32),
        blank_window,
        blank_window,
    )
    grad_q, key_window_gradient, value_window_gradient = process_tiles(back_tile, backward_start)
    term_values = jnp.stack([key_window_gradient, value_window_gradient]).reshape(
        2, window_width, KEY_VALUE_HEADS * HEAD_SIZE
    )
    summed = term_values[:, before * row_batch :]
    for dist in range(1, before + 1):
        piece = term_values[:, (before - dist) * row_batch : (before - dist + 1) * row_batch]
        summed = summed + shifted(piece, "ctx", -dist)
    attended = output_heads.reshape(row_batch, QUERY_HEADS * HEAD_SIZE)
    grad_queries = grad_q.astype(jnp.bfloat16).reshape(row_batch, QUERY_HEADS * HEAD_SIZE)
    return (attended, grad_queries, summed[0].astype(jnp.bfloat16), summed[1].astype(jnp.bfloat16))


def solution(mesh):
    return jax.shard_map(
        per_device,
        mesh=mesh,
        in_specs=(
            P(("dp", "ctx"), None),
            P(("dp", "ctx"), None),
            P(("dp", "ctx"), None),
            P(("dp", "ctx"), None),
            P("dp"),
        ),
        out_specs=(
            P(("dp", "ctx"), None),
            P(("dp", "ctx"), None),
            P(("dp", "ctx"), None),
            P(("dp", "ctx"), None),
        ),
        check_vma=False,
    )
```

profile of v0, /device:TPU:237, one launch (start us, length us, event | category | flops | bytes accessed | tf_op | source)
XLA Modules:
  0.0 92.7 jit_solution(1753568123498792419)
XLA Ops:
  0.6 1.0 %copy.64 = bf16[256,256]{0,1:T(8,128)(2,1)S(1)} copy(bf16[256,256]{1,0:T(8,128)(2,1)} %param.18) | data formatting | bytes 262144 | tf_op args[1]
  1.6 1.0 %copy.65 = bf16[256,256]{0,1:T(8,128)(2,1)S(1)} copy(bf16[256,256]{1,0:T(8,128)(2,1)} %param.19) | data formatting | bytes 262144 | tf_op args[2]
  2.7 5.1 %collective-permute-start.2 = (bf16[2,256,256]{1,2,0:T(8,128)(2,1)S(1)}, bf16[2,256,256]{1,2,0:T(8,128)(2,1)S(1)}, u32[]{:S(2)}, u32[]{:S(2)}) collective-permute-start(bf16[2,256,256]{1,2,0:T(8,128)(2,1)S(1)} %pad_maximum_fusion.1), channel_id=1, source_target_pairs={{0,1},{1,2},{2,3},{3,4},{4,5},{5,6},{6,7},{7,8},{8,9},{9,10},{10,1... | collective-permute-start | bytes 786440 | tf_op jit(solution)/shard_map/ppermute | solution.py:19
  7.8 2.6 %collective-permute-start.1 = (bf16[2,256,256]{1,2,0:T(8,128)(2,1)S(1)}, bf16[2,256,256]{1,2,0:T(8,128)(2,1)S(1)}, u32[]{:S(2)}, u32[]{:S(2)}) collective-permute-start(bf16[2,256,256]{1,2,0:T(8,128)(2,1)S(1)} %pad_maximum_fusion.1), channel_id=1, source_target_pairs={{0,2},{1,3},{2,4},{3,5},{4,6},{5,7},{6,8},{7,9},{8,10},{9,11},{10,... | collective-permute-start | bytes 786440 | tf_op jit(solution)/shard_map/ppermute | solution.py:19
  10.4 1.9 %collective-permute-start = (bf16[2,256,256]{1,2,0:T(8,128)(2,1)S(1)}, bf16[2,256,256]{1,2,0:T(8,128)(2,1)S(1)}, u32[]{:S(2)}, u32[]{:S(2)}) collective-permute-start(bf16[2,256,256]{1,2,0:T(8,128)(2,1)S(1)} %pad_maximum_fusion.1), channel_id=1, source_target_pairs={{0,3},{1,4},{2,5},{3,6},{4,7},{5,8},{6,9},{7,10},{8,11},{9,12},{10... | collective-permute-start | bytes 786440 | tf_op jit(solution)/shard_map/ppermute | solution.py:19
  12.4 0.7 copy.66
  13.5 1.5 %copy.67 = bf16[256,1792]{0,1:T(8,128)(2,1)S(1)} copy(bf16[256,1792]{1,0:T(8,128)(2,1)} %param.17) | data formatting | bytes 1835008 | tf_op args[0]
  15.0 2.2 %copy.74 = bf16[256,1792]{0,1:T(8,128)(2,1)} copy(bf16[256,1792]{1,0:T(8,128)(2,1)} %param.20) | data formatting | bytes 1835008 | tf_op args[3]
  17.9 4.5 %collective-permute-done = bf16[2,256,256]{1,2,0:T(8,128)(2,1)S(1)} collective-permute-done((bf16[2,256,256]{1,2,0:T(8,128)(2,1)S(1)}, bf16[2,256,256]{1,2,0:T(8,128)(2,1)S(1)}, u32[]{:S(2)}, u32[]{:S(2)}) %collective-permute-start) | collective-permute-done | bytes 262176 | tf_op jit(solution)/shard_map/ppermute | solution.py:19
  22.5 1.3 %fusion.11 = (f32[2,7,256]{2,1,0:T(8,128)S(1)}, f32[2,512,256,7]{2,1,3,0:T(8,128)S(1)}) fusion(pred[256,512]{0,1:T(8,128)(4,1)S(1)} %get-tuple-element.107, bf16[512,2,128,1]{0,2,3,1:T(8,128)(2,1)S(1)} %bitcast.160, bf16[256,2,7,128]{0,3,2,1:T(8,128)(2,1)S(1)} %bitcast.154), kind=kOutput, calls=%fused_computation.19 | convolution fusion | flops 475263488 | bytes 8665088 | tf_op jit(solution)/shard_map/rkgd,wkd->kgrw/dot_general | solution.py:38
  23.8 1.3 %fusion.10 = (f32[2,7,256]{2,1,0:T(8,128)S(1)}, f32[2,512,256,7]{2,1,3,0:T(8,128)S(1)}) fusion(pred[256,512]{0,1:T(8,128)(4,1)S(1)} %get-tuple-element.106, bf16[512,2,128,1]{0,2,3,1:T(8,128)(2,1)S(1)} %bitcast.162, bf16[256,2,7,128]{0,3,2,1:T(8,128)(2,1)S(1)} %bitcast.155), kind=kOutput, calls=%fused_computation.18 | convolution fusion | flops 475263488 | bytes 8665088 | tf_op jit(solution)/shard_map/rkgd,wkd->kgrw/dot_general | solution.py:38
  25.2 3.7 %select_reduce_fusion = (f32[2,7,256]{2,1,0:T(8,128)S(1)}, f32[2,7,256]{2,1,0:T(8,128)S(1)}) fusion(f32[2,512,256,7]{2,1,3,0:T(8,128)S(1)} %get-tuple-element.111, f32[2,7,256]{2,1,0:T(8,128)S(1)} %get-tuple-element.99, pred[256,512]{0,1:T(8,128)(4,1)S(1)} %get-tuple-element.107, f32[2,7,256]{2,1,0:T(8,128)S(1)} %get-tuple-element.98, ...), kind=kLoop, calls=%fused_computation.16 | loop fusion | flops 18342912 | bytes 14999552 | tf_op jit(solution)/shard_map/reduce_sum | solution.py:89
  29.0 1.6 %convolution_bitcast_fusion.1 = f32[512,2,128]{0,2,1:T(8,128)S(1)} fusion(bf16[256,2,7,128]{0,3,2,1:T(8,128)(2,1)S(1)} %bitcast.168, f32[2,512,256,7]{2,1,3,0:T(8,128)S(1)} %get-tuple-element.109, f32[2,7,256]{2,1,0:T(8,128)S(1)} %log_add_fusion, pred[256,512]{0,1:T(8,128)(4,1)S(1)} %get-tuple-element.106), kind=kOutput, calls=%fused_computation.28 | convolution fusion | flops 477102080 | bytes 8927232 | tf_op jit(solution)/shard_map/cmsl,scme->lce/dot_general | solution.py:151
  30.6 1.8 %fusion.17 = f32[2,128,7,256]{3,1,2,0:T(8,128)S(1)} fusion(bf16[512,2,128,1]{0,2,3,1:T(8,128)(2,1)S(1)} %bitcast.174, f32[2,512,256,7]{2,1,3,0:T(8,128)S(1)} %get-tuple-element.111, f32[2,7,256]{2,1,0:T(8,128)S(1)} %log_add_fusion, pred[256,512]{0,1:T(8,128)(4,1)S(1)} %get-tuple-element.107), kind=kOutput, calls=%fused_computation.43 | convolution fusion | flops 477102080 | bytes 9582592 | tf_op jit(solution)/shard_map/kgrw,wkd->rkgd/dot_general | solution.py:115
  32.5 2.8 %multiply_reduce_fusion = (f32[256,2,7]{0,2,1:T(8,128)S(1)}, bf16[2,128,7,256]{3,1,2,0:T(8,128)(2,1)}) fusion(bf16[256,2,7,128]{0,3,2,1:T(8,128)(2,1)S(1)} %bitcast.169, f32[2,128,7,256]{3,1,2,0:T(8,128)S(1)} %fusion.17, bf16[512,2,128,1]{0,2,3,1:T(8,128)(2,1)S(1)} %bitcast.176, f32[2,512,256,7]{2,1,3,0:T(8,128)S(1)} %get-tuple-element.109, ...), kind=kOutput, calls=%fused_computation.24 | convolution fusion | flops 479851008 | bytes 11431936 | tf_op jit(solution)/shard_map/kgrw,wkd->rkgd/dot_general | solution.py:115
  35.3 2.8 %fusion.2 = bf16[2,7,256,512]{2,3,1,0:T(8,128)(2,1)S(1)} fusion(f32[2,512,256,7]{2,1,3,0:T(8,128)S(1)} %get-tuple-element.111, f32[2,7,256]{2,1,0:T(8,128)S(1)} %bitcast.179, f32[2,7,256]{2,1,0:T(8,128)S(1)} %log_add_fusion, pred[256,512]{0,1:T(8,128)(4,1)S(1)} %get-tuple-element.107, bf16[512,2,128,1]{0,2,3,1:T(8,128)(2,1)S(1)} %bitcast.175, ...), kind=kOutput, calls=%fused_computation.3 | convolution fusion | flops 482607104 | bytes 12349440 | tf_op jit(solution)/shard_map/rkgd,wkd->kgrw/dot_general | solution.py:46
  38.1 3.0 %fusion.5 = bf16[2,7,256,512]{2,3,1,0:T(8,128)(2,1)S(1)} fusion(f32[2,512,256,7]{2,1,3,0:T(8,128)S(1)} %get-tuple-element.109, f32[2,7,256]{2,1,0:T(8,128)S(1)} %bitcast.180, f32[2,7,256]{2,1,0:T(8,128)S(1)} %log_add_fusion, pred[256,512]{0,1:T(8,128)(4,1)S(1)} %get-tuple-element.106, bf16[512,2,128,1]{0,2,3,1:T(8,128)(2,1)S(1)} %bitcast.177, ...), kind=kOutput, calls=%fused_computation.7 | convolution fusion | flops 482607104 | bytes 12349440 | tf_op jit(solution)/shard_map/rkgd,wkd->kgrw/dot_general | solution.py:46
  41.2 1.7 %fusion.14 = f32[1,1024,2,128]{1,3,2,0:T(8,128)S(1)} fusion(f32[1,1024,2,128]{1,3,2,0:T(8,128)S(1)} %pad_bitcast_fusion, bf16[256,2,7,128]{0,3,2,1:T(8,128)(2,1)S(1)} %bitcast.172, f32[2,512,256,7]{2,1,3,0:T(8,128)S(1)} %get-tuple-element.111, f32[2,7,256]{2,1,0:T(8,128)S(1)} %log_add_fusion, pred[256,512]{0,1:T(8,128)(4,1)S(1)} %get-tuple-element.107), kind=kOutput, calls=%fused_computation.27 | convolution fusion | flops 477102080 | bytes 8929280 | tf_op jit(solution)/shard_map/cmsl,scme->lce/dot_general | solution.py:151
  42.8 1.3 %convolution_bitcast_fusion.3 = f32[512,2,128]{0,2,1:T(8,128)S(1)} fusion(bf16[2,7,256,512]{2,3,1,0:T(8,128)(2,1)S(1)} %fusion.5, bf16[256,2,7,128]{0,3,2,1:T(8,128)(2,1)S(1)} %bitcast.156), kind=kOutput, calls=%fused_computation.31 | convolution fusion | flops 469762048 | bytes 5111808 | tf_op jit(solution)/shard_map/cmsl,scme->lce/dot_general | solution.py:146
  44.3 1.3 %fusion.15 = f32[1,1024,2,128]{1,3,2,0:T(8,128)S(1)} fusion(f32[1,1024,2,128]{1,3,2,0:T(8,128)S(1)} %pad_bitcast_fusion.1, bf16[2,7,256,512]{2,3,1,0:T(8,128)(2,1)S(1)} %fusion.2, bf16[256,2,7,128]{0,3,2,1:T(8,128)(2,1)S(1)} %bitcast.157), kind=kOutput, calls=%fused_computation.30 | convolution fusion | flops 469762048 | bytes 5111808 | tf_op jit(solution)/shard_map/cmsl,scme->lce/dot_general | solution.py:146
  45.9 1.0 %copy.124 = f32[2,256,256]{2,1,0:T(8,128)} copy(f32[2,256,256]{1,2,0:T(8,128)S(1)} %get-tuple-element.88) | data formatting | bytes 1048576
  46.9 1.0 %copy.125 = f32[2,256,256]{2,1,0:T(8,128)} copy(f32[2,256,256]{1,2,0:T(8,128)S(1)} %get-tuple-element.89) | data formatting | bytes 1048576
  48.0 1.0 %copy.126 = f32[2,256,256]{2,1,0:T(8,128)} copy(f32[2,256,256]{1,2,0:T(8,128)S(1)} %get-tuple-element.91) | data formatting | bytes 1048576
  49.0 3.0 %collective-permute-start.5 = (f32[2,256,256]{2,1,0:T(8,128)}, f32[2,256,256]{2,1,0:T(8,128)}, u32[]{:S(2)}, u32[]{:S(2)}) collective-permute-start(f32[2,256,256]{2,1,0:T(8,128)} %copy.126), channel_id=1, source_target_pairs={{3,0},{4,1},{5,2},{6,3},{7,4},{8,5},{9,6},{10,7},{11,8},{12,9},{13... | collective-permute-start | bytes 1572872 | tf_op jit(solution)/shard_map/ppermute | solution.py:19
  52.0 4.8 %collective-permute-start.4 = (f32[2,256,256]{2,1,0:T(8,128)}, f32[2,256,256]{2,1,0:T(8,128)}, u32[]{:S(2)}, u32[]{:S(2)}) collective-permute-start(f32[2,256,256]{2,1,0:T(8,128)} %copy.125), channel_id=1, source_target_pairs={{2,0},{3,1},{4,2},{5,3},{6,4},{7,5},{8,6},{9,7},{10,8},{11,9},{12,... | collective-permute-start | bytes 1572872 | tf_op jit(solution)/shard_map/ppermute | solution.py:19
  56.8 2.3 %collective-permute-start.3 = (f32[2,256,256]{2,1,0:T(8,128)}, f32[2,256,256]{2,1,0:T(8,128)}, u32[]{:S(2)}, u32[]{:S(2)}) collective-permute-start(f32[2,256,256]{2,1,0:T(8,128)} %copy.124), channel_id=1, source_target_pairs={{1,0},{2,1},{3,2},{4,3},{5,4},{6,5},{7,6},{8,7},{9,8},{10,9},{11,1... | collective-permute-start | bytes 1572872 | tf_op jit(solution)/shard_map/ppermute | solution.py:19
  59.1 2.7 %fusion.35 = f32[2,128,7,256]{3,1,2,0:T(8,128)S(1)} fusion(bf16[512,2,128,1]{0,2,3,1:T(8,128)(2,1)S(1)} %bitcast.161, bf16[2,7,256,512]{2,3,1,0:T(8,128)(2,1)} %copy-done.1), kind=kOutput, calls=%fused_computation.66 | convolution fusion | flops 469762048 | bytes 5767168 | tf_op jit(solution)/shard_map/kgrw,wkd->rkgd/dot_general | solution.py:142
  61.8 2.2 %copy.89 = bf16[256,1792]{1,0:T(8,128)(2,1)} copy(bf16[256,1792]{0,1:T(8,128)(2,1)} %bitcast.173) | data formatting | bytes 1835008
  64.0 2.7 %add_convert_fusion = bf16[2,128,7,256]{3,1,2,0:T(8,128)(2,1)S(1)} fusion(f32[2,128,7,256]{3,1,2,0:T(8,128)S(1)} %fusion.35, bf16[512,2,128,1]{0,2,3,1:T(8,128)(2,1)S(1)} %bitcast.163, bf16[2,7,256,512]{2,3,1,0:T(8,128)(2,1)} %copy-done), kind=kOutput, calls=%fused_computation.23 | convolution fusion | flops 470679552 | bytes 6684672 | tf_op jit(solution)/shard_map/kgrw,wkd->rkgd/dot_general | solution.py:142
  66.7 1.4 %copy.90 = bf16[256,1792]{1,0:T(8,128)(2,1)} copy(bf16[256,1792]{0,1:T(8,128)(2,1)S(1)} %bitcast.159) | data formatting | bytes 1835008
  68.3 22.2 %collective-permute-done.5 = f32[2,256,256]{2,1,0:T(8,128)} collective-permute-done((f32[2,256,256]{2,1,0:T(8,128)}, f32[2,256,256]{2,1,0:T(8,128)}, u32[]{:S(2)}, u32[]{:S(2)}) %collective-permute-start.5) | collective-permute-done | bytes 524320 | tf_op jit(solution)/shard_map/ppermute | solution.py:19
  90.5 1.5 %add_convert_fusion.2 = bf16[2,256,256]{2,1,0:T(8,128)(2,1)S(1)} fusion(f32[2,256,256]{2,1,0:T(8,128)} %collective-permute-done.5, f32[2,256,256]{2,1,0:T(8,128)} %collective-permute-done.4, f32[2,256,256]{2,1,0:T(8,128)S(1)} %copy.123, f32[2,256,256]{2,1,0:T(8,128)} %collective-permute-done.3), kind=kLoop, calls=%fused_computation.35 | loop fusion | flops 524288 | bytes 2359296 | tf_op jit(solution)/shard_map/convert.1
  (34 shorter events, 2.7 us)
Async XLA Ops:
  2.7 15.2 %collective-permute-start.2 = (bf16[2,256,256]{1,2,0:T(8,128)(2,1)S(1)}, bf16[2,256,256]{1,2,0:T(8,128)(2,1)S(1)}, u32[]{:S(2)}, u32[]{:S(2)}) collective-permute-start(bf16[2,256,256]{1,2,0:T(8,128)(2,1)S(1)} %pad_maximum_fusion.1), channel_id=1, source_target_pairs={{0,1},{1,2},{2,3},{3,4},{4,5},{5,6},{6,7},{7,8},{8,9},{9,10},{10,1... | collective-permute-start | bytes 786440 | tf_op jit(solution)/shard_map/ppermute | solution.py:19
  7.8 14.6 %collective-permute-start.1 = (bf16[2,256,256]{1,2,0:T(8,128)(2,1)S(1)}, bf16[2,256,256]{1,2,0:T(8,128)(2,1)S(1)}, u32[]{:S(2)}, u32[]{:S(2)}) collective-permute-start(bf16[2,256,256]{1,2,0:T(8,128)(2,1)S(1)} %pad_maximum_fusion.1), channel_id=1, source_target_pairs={{0,2},{1,3},{2,4},{3,5},{4,6},{5,7},{6,8},{7,9},{8,10},{9,11},{10,... | collective-permute-start | bytes 786440 | tf_op jit(solution)/shard_map/ppermute | solution.py:19
  10.4 11.9 %collective-permute-start = (bf16[2,256,256]{1,2,0:T(8,128)(2,1)S(1)}, bf16[2,256,256]{1,2,0:T(8,128)(2,1)S(1)}, u32[]{:S(2)}, u32[]{:S(2)}) collective-permute-start(bf16[2,256,256]{1,2,0:T(8,128)(2,1)S(1)} %pad_maximum_fusion.1), channel_id=1, source_target_pairs={{0,3},{1,4},{2,5},{3,6},{4,7},{5,8},{6,9},{7,10},{8,11},{9,12},{10... | collective-permute-start | bytes 786440 | tf_op jit(solution)/shard_map/ppermute | solution.py:19
  25.2 3.8 %copy-start.2 = (bf16[256,1792]{0,1:T(8,128)(2,1)S(1)}, bf16[256,1792]{0,1:T(8,128)(2,1)}, u32[]{:S(2)}) copy-start(bf16[256,1792]{0,1:T(8,128)(2,1)} %copy.74) | copy-start | bytes 2752516
  38.1 6.2 %copy-start.1 = (bf16[2,7,256,512]{2,3,1,0:T(8,128)(2,1)}, bf16[2,7,256,512]{2,3,1,0:T(8,128)(2,1)S(1)}, u32[]{:S(2)}) copy-start(bf16[2,7,256,512]{2,3,1,0:T(8,128)(2,1)S(1)} %fusion.2) | copy-start | bytes 11010052
  41.1 3.1 %copy-start = (bf16[2,7,256,512]{2,3,1,0:T(8,128)(2,1)}, bf16[2,7,256,512]{2,3,1,0:T(8,128)(2,1)S(1)}, u32[]{:S(2)}) copy-start(bf16[2,7,256,512]{2,3,1,0:T(8,128)(2,1)S(1)} %fusion.5) | copy-start | bytes 11010052
  49.0 41.5 %collective-permute-start.5 = (f32[2,256,256]{2,1,0:T(8,128)}, f32[2,256,256]{2,1,0:T(8,128)}, u32[]{:S(2)}, u32[]{:S(2)}) collective-permute-start(f32[2,256,256]{2,1,0:T(8,128)} %copy.126), channel_id=1, source_target_pairs={{3,0},{4,1},{5,2},{6,3},{7,4},{8,5},{9,6},{10,7},{11,8},{12,9},{13... | collective-permute-start | bytes 1572872 | tf_op jit(solution)/shard_map/ppermute | solution.py:19
  52.0 38.5 %collective-permute-start.4 = (f32[2,256,256]{2,1,0:T(8,128)}, f32[2,256,256]{2,1,0:T(8,128)}, u32[]{:S(2)}, u32[]{:S(2)}) collective-permute-start(f32[2,256,256]{2,1,0:T(8,128)} %copy.125), channel_id=1, source_target_pairs={{2,0},{3,1},{4,2},{5,3},{6,4},{7,5},{8,6},{9,7},{10,8},{11,9},{12,... | collective-permute-start | bytes 1572872 | tf_op jit(solution)/shard_map/ppermute | solution.py:19
  56.8 33.7 %collective-permute-start.3 = (f32[2,256,256]{2,1,0:T(8,128)}, f32[2,256,256]{2,1,0:T(8,128)}, u32[]{:S(2)}, u32[]{:S(2)}) collective-permute-start(f32[2,256,256]{2,1,0:T(8,128)} %copy.124), channel_id=1, source_target_pairs={{1,0},{2,1},{3,2},{4,3},{5,4},{6,5},{7,6},{8,7},{9,8},{10,9},{11,1... | collective-permute-start | bytes 1572872 | tf_op jit(solution)/shard_map/ppermute | solution.py:19
where the time goes:
time: 93.1 us; the launch traced here: 92.7 us
  waiting for transfers between devices  26.7 us (29%)
  matrix products  24.3 us (26%)
  starting transfers between devices  19.8 us (21%)
  local copies, waits for them, and re-layouts  14.5 us (16%)
  other arithmetic  6.42 us (7%)
  between operations  1.02 us (1%)
    ppermute x6, waiting for transfers between devices, shifted(): return lax.ppermute(value, axis, pairs)  26.7 us
    ppermute x6, starting transfers between devices, shifted(): return lax.ppermute(value, axis, pairs)  19.8 us
    unnamed x17, local copies, waits for them, and re-layouts  12.5 us
    dot_general x2, matrix products, grad_terms(): jnp.einsum('rkgd,wkd->kgrw', heads_gradient, v_tile, preferred_element_ty...  5.76 us
    dot_general x2, matrix products, back_tile(): jnp.einsum('kgrw,wkd->rkgd', score_gradient, k_tile, preferred_element_ty...  5.38 us
    dot_general x2, matrix products, output_tile(): jnp.einsum('kgrw,wkd->rkgd', probs, window_values[low_end:low_end + tile]...  4.63 us
    reduce_sum x1, other arithmetic, stats_tile(): jnp.sum(jnp.where(mask, jnp.exp(scores - new_top[..., None]), 0.0), axis=-1)  3.73 us
    dot_general x2, matrix products, back_tile(): jnp.einsum('cmsl,scme->lce', lower_bound, heads_gradient, preferred_eleme...  3.29 us
  transfers between devices with their start and end apart: 6, of which 2 were waited for; matrix products, arithmetic and copies ran while one was open for 16% of the time, Pallas kernels for 0%

commit v1 on v0

v1 whole, which is shorter than its diff:
```python
import math

import jax
import jax.numpy as jnp
from jax import lax
from jax.experimental import pallas as pl
from jax.experimental.pallas import tpu as pltpu
from jax.sharding import PartitionSpec as P

QUERY_HEADS = 14
KEY_VALUE_HEADS = 2
HEAD = 128
GROUP = QUERY_HEADS // KEY_VALUE_HEADS
DOCS = 32
ROWS = 256
HALO = 3
WINDOW = (HALO + 1) * ROWS
NEGATIVE_FILL = -1e30
SCALE = 1.0 / math.sqrt(HEAD)
LOG2E_SCALE = math.log2(math.e) * SCALE
BF16 = jnp.bfloat16
F32 = jnp.float32
MESH = pl.DeviceIdType.MESH
VMEM = pl.BlockSpec(memory_space=pltpu.VMEM)
SMEM = pl.BlockSpec(memory_space=pltpu.SMEM)
ANY = pl.BlockSpec(memory_space=pl.ANY)


def dot_nn(a, b):
    return lax.dot_general(a, b, (((1,), (0,)), ((), ())), preferred_element_type=F32)


def dot_nt(a, b):
    return lax.dot_general(a, b, (((1,), (1,)), ((), ())), preferred_element_type=F32)


def ring(me, by, count):
    return lax.rem(me + by + count, count)


def greet(me, count, offsets):
    barrier = pltpu.get_barrier_semaphore()
    for by in offsets:
        pl.semaphore_signal(
            barrier, inc=1, device_id={"ctx": ring(me, by, count)}, device_id_type=MESH
        )
    pl.semaphore_wait(barrier, len(offsets))


def remote(src, dst, send, recv, target):
    return pltpu.make_async_remote_copy(
        src_ref=src,
        dst_ref=dst,
        send_sem=send,
        recv_sem=recv,
        device_id={"ctx": target},
        device_id_type=MESH,
    )


def gather_kernel(count, k_ref, v_ref, halo_ref, send_sem, recv_sem):
    me = lax.axis_index("ctx")
    core = lax.rem(me, 2)
    greet(me, count, (-2, -1, 1, 2))
    own = (k_ref, v_ref)
    ahead = [
        remote(own[c], halo_ref.at[1, c], send_sem.at[0, c], recv_sem.at[1, c], ring(me, 2, count))
        for c in range(2)
    ]
    for copy in ahead:
        copy.start()
    beside = [
        remote(own[c], halo_ref.at[0, c], send_sem.at[1, c], recv_sem.at[0, c], ring(me, 1, count))
        for c in range(2)
    ]
    to_next = [
        remote(
            halo_ref.at[1, c],
            halo_ref.at[2, c],
            send_sem.at[2, c],
            recv_sem.at[2, c],
            ring(me, 1, count),
        )
        for c in range(2)
    ]
    to_partner = [
        remote(
            halo_ref.at[1, c],
            halo_ref.at[0, c],
            send_sem.at[1, c],
            recv_sem.at[0, c],
            ring(me, -1, count),
        )
        for c in range(2)
    ]

    @pl.when(core == 0)
    def _():
        for copy in beside:
            copy.start()

    for c in range(2):
        ahead[c].wait_recv()
        to_next[c].start()

        @pl.when(core == 1)
        def _():
            to_partner[c].start()

    for c in range(2):
        beside[c].wait_recv()
        to_next[c].wait_recv()
        ahead[c].wait_send()
        beside[c].wait_send()
        to_next[c].wait_send()


def attention_kernel(
    len_ref, q_ref, k_ref, v_ref, halo_ref, do_ref,
    o_ref, dq_ref, part_ref, own_ref,
    bias, kw, vw, kt, vt, e_all, ds_all, q_all, do_all, s_buf,
):
    me = lax.axis_index("ctx")
    base = me * ROWS
    q_pos = base + lax.broadcasted_iota(jnp.int32, (1, ROWS), 1)
    start = jnp.zeros((1, ROWS), jnp.int32)
    total = jnp.int32(0)
    for d in range(DOCS):
        total = total + len_ref[d]
        start = jnp.where(q_pos >= total, total, start)
    k_pos = base - HALO * ROWS + lax.broadcasted_iota(jnp.int32, (WINDOW, ROWS), 0)
    bias[...] = jnp.where((k_pos <= q_pos) & (k_pos >= start), 0.0, NEGATIVE_FILL)
    for g in range(KEY_VALUE_HEADS):
        cols = slice(g * HEAD, (g + 1) * HEAD)
        for d in range(HALO):
            rows = slice((HALO - 1 - d) * ROWS, (HALO - d) * ROWS)
            kw[g, rows] = halo_ref[d, 0, :, cols]
            vw[g, rows] = halo_ref[d, 1, :, cols]
        kw[g, HALO * ROWS :] = k_ref[:, cols]
        vw[g, HALO * ROWS :] = v_ref[:, cols]
        kt[g] = kw[g].T
        vt[g] = vw[g].T

    def scores(h, live):
        g, slot = h // GROUP, h % GROUP
        cols = slice(h * HEAD, (h + 1) * HEAD)
        q_t = q_ref[:, cols].T
        q_all[h] = q_t
        s = dot_nn(kw[g], q_t) + bias[...]
        s_buf[h % 2] = s
        live["m"] = jnp.max(s, axis=0, keepdims=True)

    def soft(h, live):
        e = jnp.exp2((s_buf[h % 2] - live["m"]) * LOG2E_SCALE)
        live["r"] = 1.0 / jnp.sum(e, axis=0, keepdims=True)
        e_all[h] = e.astype(BF16)

    def out(h, live):
        g = h // GROUP
        cols = slice(h * HEAD, (h + 1) * HEAD)
        o_t = (dot_nn(vt[g], e_all[h]) * live["r"]).astype(BF16)
        o_ref[:, cols] = o_t.T
        do_t = do_ref[:, cols].T.astype(F32)
        live["delta"] = jnp.sum(do_t * o_t.astype(F32), axis=0, keepdims=True) * live["r"]
        do_all[h] = (do_t * live["r"]).astype(BF16)

    def back(h, live):
        g = h // GROUP
        dp = dot_nn(vw[g], do_all[h])
        ds_all[h] = (e_all[h].astype(F32) * (dp - live["delta"])).astype(BF16)

    def grad_q(h, live):
        g = h // GROUP
        cols = slice(h * HEAD, (h + 1) * HEAD)
        dq_ref[:, cols] = (dot_nn(kt[g], ds_all[h]) * SCALE).astype(BF16).T

    stages = (scores, soft, out, back, grad_q)
    lives = [dict() for _ in range(QUERY_HEADS)]
    for step in range(QUERY_HEADS + len(stages) - 1):
        for lag, stage in enumerate(stages):
            if 0 <= step - lag < QUERY_HEADS:
                stage(step - lag, lives[step - lag])

    for g in range(KEY_VALUE_HEADS):
        cols = slice(g * HEAD, (g + 1) * HEAD)
        for b in range(HALO + 1):
            rows = slice(b * ROWS, (b + 1) * ROWS)
            grad_k = jnp.zeros((ROWS, HEAD), F32)
            grad_v = jnp.zeros((ROWS, HEAD), F32)
            for h in range(g * GROUP, (g + 1) * GROUP):
                grad_k += dot_nt(ds_all[h, rows], q_all[h])
                grad_v += dot_nt(e_all[h, rows], do_all[h])
            if b == HALO:
                own_ref[0, :, cols] = grad_k * SCALE
                own_ref[1, :, cols] = grad_v
            else:
                part_ref[HALO - 1 - b, 0, :, cols] = (grad_k * SCALE).astype(BF16)
                part_ref[HALO - 1 - b, 1, :, cols] = grad_v.astype(BF16)


def scatter_kernel(
    count, part_ref, own_ref, gk_ref, gv_ref,
    total, from_partner, from_next, direct, back, send_sem, recv_sem,
):
    me = lax.axis_index("ctx")
    core = lax.rem(me, 2)
    greet(me, count, (-3, -2, -1, 1, 2, 3))
    chunks = [(c, pl.ds(r * 128, 128)) for c in range(2) for r in range(2)]
    grads = (gk_ref, gv_ref)

    @pl.when(core == 0)
    def _():
        relay, partner, last = [], [], []
        for n, (c, rows) in enumerate(chunks):
            relay.append(
                remote(
                    part_ref.at[2, c, rows], from_next.at[c, rows],
                    send_sem.at[0, n], recv_sem.at[0, n], ring(me, -2, count),
                )
            )
            partner.append(
                remote(
                    part_ref.at[1, c, rows], from_partner.at[c, rows],
                    send_sem.at[1, n], recv_sem.at[1, n], ring(me, 1, count),
                )
            )
            last.append(
                remote(
                    total.at[c, rows], back.at[c, rows],
                    send_sem.at[2, n], recv_sem.at[2, n], ring(me, -1, count),
                )
            )
            partner[n].start()
            relay[n].start()
        for n, (c, rows) in enumerate(chunks):
            partner[n].wait_recv()
            relay[n].wait_recv()
            total[c, rows] = (
                part_ref[0, c, rows].astype(F32)
                + from_partner[c, rows].astype(F32)
                + from_next[c, rows].astype(F32)
            ).astype(BF16)
            last[n].start()
        for n, (c, rows) in enumerate(chunks):
            remote(
                total.at[c, rows], direct.at[c, rows],
                send_sem.at[3, n], recv_sem.at[3, n], ring(me, 1, count),
            ).wait_recv()
            last[n].wait_recv()
            grads[c][rows, :] = (
                own_ref[c, rows] + direct[c, rows].astype(F32) + back[c, rows].astype(F32)
            ).astype(BF16)
        for n in range(len(chunks)):
            relay[n].wait_send()
            partner[n].wait_send()
            last[n].wait_send()

    @pl.when(core == 1)
    def _():
        first, partner, last = [], [], []
        for n, (c, rows) in enumerate(chunks):
            first.append(
                remote(
                    part_ref.at[0, c, rows], direct.at[c, rows],
                    send_sem.at[3, n], recv_sem.at[3, n], ring(me, -1, count),
                )
            )
            partner.append(
                remote(
                    part_ref.at[1, c, rows], from_partner.at[c, rows],
                    send_sem.at[1, n], recv_sem.at[1, n], ring(me, -1, count),
                )
            )
            last.append(
                remote(
                    total.at[c, rows], back.at[c, rows],
                    send_sem.at[2, n], recv_sem.at[2, n], ring(me, -3, count),
                )
            )
            partner[n].start()
        for n, (c, rows) in enumerate(chunks):
            partner[n].wait_recv()
            total[c, rows] = (
                part_ref[2, c, rows].astype(F32) + from_partner[c, rows].astype(F32)
            ).astype(BF16)
            last[n].start()
        for n in range(len(chunks)):
            first[n].start()
        for n, (c, rows) in enumerate(chunks):
            last[n].wait_recv()
            grads[c][rows, :] = (own_ref[c, rows] + back[c, rows].astype(F32)).astype(BF16)
        for n in range(len(chunks)):
            first[n].wait_send()
            partner[n].wait_send()
            last[n].wait_send()


def per_device(queries, keys, values, output_gradient, lengths):
    count = lax.axis_size("ctx")
    width = KEY_VALUE_HEADS * HEAD
    wide = QUERY_HEADS * HEAD
    halo = pl.pallas_call(
        lambda *refs: gather_kernel(count, *refs),
        out_shape=jax.ShapeDtypeStruct((HALO, 2, ROWS, width), BF16),
        in_specs=[ANY, ANY],
        out_specs=ANY,
        scratch_shapes=[pltpu.SemaphoreType.DMA((3, 2)), pltpu.SemaphoreType.DMA((3, 2))],
        compiler_params=pltpu.CompilerParams(collective_id=0, has_side_effects=True),
        name="gather_halo",
    )(keys, values)
    attended, grad_queries, part, own = pl.pallas_call(
        attention_kernel,
        out_shape=[
            jax.ShapeDtypeStruct((ROWS, wide), BF16),
            jax.ShapeDtypeStruct((ROWS, wide), BF16),
            jax.ShapeDtypeStruct((HALO, 2, ROWS, width), BF16),
            jax.ShapeDtypeStruct((2, ROWS, width), F32),
        ],
        in_specs=[SMEM] + [VMEM] * 5,
        out_specs=[VMEM] * 4,
        scratch_shapes=[
            pltpu.VMEM((WINDOW, ROWS), F32),
            pltpu.VMEM((KEY_VALUE_HEADS, WINDOW, HEAD), BF16),
            pltpu.VMEM((KEY_VALUE_HEADS, WINDOW, HEAD), BF16),
            pltpu.VMEM((KEY_VALUE_HEADS, HEAD, WINDOW), BF16),
            pltpu.VMEM((KEY_VALUE_HEADS, HEAD, WINDOW), BF16),
            pltpu.VMEM((QUERY_HEADS, WINDOW, ROWS), BF16),
            pltpu.VMEM((QUERY_HEADS, WINDOW, ROWS), BF16),
            pltpu.VMEM((QUERY_HEADS, HEAD, ROWS), BF16),
            pltpu.VMEM((QUERY_HEADS, HEAD, ROWS), BF16),
            pltpu.VMEM((2, WINDOW, ROWS), F32),
        ],
        compiler_params=pltpu.CompilerParams(vmem_limit_bytes=56 << 20),
        name="attention",
    )(lengths, queries, keys, values, halo, output_gradient)
    grad_keys, grad_values = pl.pallas_call(
        lambda *refs: scatter_kernel(count, *refs),
        out_shape=[jax.ShapeDtypeStruct((ROWS, width), BF16)] * 2,
        in_specs=[VMEM, VMEM],
        out_specs=[VMEM, VMEM],
        scratch_shapes=[pltpu.VMEM((2, ROWS, width), BF16)] * 5
        + [pltpu.SemaphoreType.DMA((4, 4)), pltpu.SemaphoreType.DMA((4, 4))],
        compiler_params=pltpu.CompilerParams(
            collective_id=1, has_side_effects=True, vmem_limit_bytes=32 << 20
        ),
        name="scatter_gradients",
    )(part, own)
    return attended, grad_queries, grad_keys, grad_values


def solution(mesh):
    split = P(("dp", "ctx"), None)
    return jax.shard_map(
        per_device,
        mesh=mesh,
        in_specs=(split, split, split, split, P("dp")),
        out_specs=(split, split, split, split),
        check_vma=False,
    )
```

time: 93.1 us -> 52.2 us (0.56)
  the two profiles are of different devices: /device:TPU:237 before, /device:TPU:1 now
where the time goes in v1:
time: 52.2 us; the launch traced here: 52 us
  Pallas kernels  47.9 us (92%)
  local copies, waits for them, and re-layouts  3.49 us (7%)
  between operations  0.65 us (1%)
    pallas_call x1, Pallas kernels, per_device(): pl.pallas_call(lambda *refs: gather_kernel(count, *refs), out_shape=jax.S...  18 us
    pallas_call x1, Pallas kernels, per_device(): pl.pallas_call(attention_kernel, out_shape=[jax.ShapeDtypeStruct((ROWS, w...  16.2 us
    pallas_call x1, Pallas kernels, per_device(): pl.pallas_call(lambda *refs: scatter_kernel(count, *refs), out_shape=[jax...  13.6 us
    unnamed x6, local copies, waits for them, and re-layouts  3.49 us

profile of v1, /device:TPU:1, one launch (start us, length us, event | category | flops | bytes accessed | tf_op | source)
XLA Modules:
  0.0 52.0 jit_solution(5422679189656152989)
XLA Ops:
  0.6 18.0 %gather_halo.1.halo_ref = bf16[3,2,256,256]{3,2,1,0:T(8,128)(2,1)} custom-call(bf16[256,256]{1,0:T(8,128)(2,1)} %k_ref.1, bf16[256,256]{1,0:T(8,128)(2,1)} %v_ref.1), custom_call_target="tpu_custom_call" | custom-call | tf_op jit(solution)/shard_map/gather_halo/pallas_call | solution.py:302
  18.7 16.2 %attention.1 = (bf16[256,1792]{1,0:T(8,128)(2,1)}, bf16[256,1792]{1,0:T(8,128)(2,1)}, bf16[3,2,256,256]{3,2,1,0:T(8,128)(2,1)}, f32[2,256,256]{2,1,0:T(8,128)}) custom-call(s32[32]{0:T(128)} %len_ref.1, bf16[256,1792]{1,0:T(8,128)(2,1)} %q_ref.1, bf16[256,256]{1,0:T(8,128)(2,1)} %k_ref.1, bf16[256,256]{1,0:T(8,128)(2,1)} %v_ref.1, ...), custom_call_target="tpu_custom_call" | custom-call | tf_op jit(solution)/shard_map/attention/pallas_call | solution.py:311
  34.9 0.0 copy-start
  34.9 1.1 %copy-done = bf16[3,2,256,256]{3,2,1,0:T(8,128)(2,1)S(1)} copy-done((bf16[3,2,256,256]{3,2,1,0:T(8,128)(2,1)S(1)}, bf16[3,2,256,256]{3,2,1,0:T(8,128)(2,1)}, u32[]{:S(2)}) %copy-start) | copy-done | bytes 786456
  36.0 0.0 copy-start.1
  36.0 1.0 %copy-done.1 = f32[2,256,256]{2,1,0:T(8,128)S(1)} copy-done((f32[2,256,256]{2,1,0:T(8,128)S(1)}, f32[2,256,256]{2,1,0:T(8,128)}, u32[]{:S(2)}) %copy-start.1) | copy-done | bytes 524312
  37.1 13.6 %scatter_gradients.1 = (bf16[256,256]{1,0:T(8,128)(2,1)S(1)}, bf16[256,256]{1,0:T(8,128)(2,1)S(1)}) custom-call(bf16[3,2,256,256]{3,2,1,0:T(8,128)(2,1)S(1)} %copy-done, f32[2,256,256]{2,1,0:T(8,128)S(1)} %copy-done.1), custom_call_target="tpu_custom_call" | custom-call | tf_op jit(solution)/shard_map/scatter_gradients/pallas_call | solution.py:336
  50.7 0.7 %copy.11 = bf16[256,256]{1,0:T(8,128)(2,1)} copy(bf16[256,256]{1,0:T(8,128)(2,1)S(1)} %get-tuple-element.22) | data formatting | bytes 262144
  51.3 0.7 %copy.12 = bf16[256,256]{1,0:T(8,128)(2,1)} copy(bf16[256,256]{1,0:T(8,128)(2,1)S(1)} %get-tuple-element.23) | data formatting | bytes 262144
Async XLA Ops:
  34.9 1.1 %copy-start = (bf16[3,2,256,256]{3,2,1,0:T(8,128)(2,1)S(1)}, bf16[3,2,256,256]{3,2,1,0:T(8,128)(2,1)}, u32[]{:S(2)}) copy-start(bf16[3,2,256,256]{3,2,1,0:T(8,128)(2,1)} %get-tuple-element.12.refs_0_) | copy-start | bytes 2359300
  36.0 1.0 %copy-start.1 = (f32[2,256,256]{2,1,0:T(8,128)S(1)}, f32[2,256,256]{2,1,0:T(8,128)}, u32[]{:S(2)}) copy-start(f32[2,256,256]{2,1,0:T(8,128)} %get-tuple-element.13.refs_1_) | copy-start | bytes 1572868

commit v2 on v0

v2 whole, which is shorter than its diff:
```python
import functools
import math

import jax
import jax.numpy as jnp
from jax import lax
from jax.experimental import pallas as pl
from jax.experimental.pallas import tpu as pltpu
from jax.sharding import PartitionSpec as P

QUERY_HEADS = 14
KEY_VALUE_HEADS = 2
HEAD = 128
GROUP = QUERY_HEADS // KEY_VALUE_HEADS
SPAN = GROUP * HEAD
DOCS = 32
ROWS = 256
SLOTS = 5
PIECES = 4
PIECE_ROWS = ROWS // 2
NEGATIVE_FILL = -1e30
SCALE = 1.0 / math.sqrt(HEAD)
LOG2E_SCALE = math.log2(math.e) * SCALE
BF16 = jnp.bfloat16
F32 = jnp.float32
MESH = pl.DeviceIdType.MESH
SMEM = pl.BlockSpec(memory_space=pltpu.SMEM)
HBM = pl.BlockSpec(memory_space=pltpu.HBM)


def dot_nn(a, b):
    return lax.dot_general(a, b, (((1,), (0,)), ((), ())), preferred_element_type=F32)


def remote(src, dst, send, recv, target):
    return pltpu.make_async_remote_copy(
        src_ref=src, dst_ref=dst, send_sem=send, recv_sem=recv,
        device_id={"ctx": target}, device_id_type=MESH,
    )


def fused_kernel(
    count, len_ref, q_ref, k_ref, v_ref, do_ref,
    o_ref, dq_ref, gk_ref, gv_ref,
    kv, kv_t, q_nat, do_nat, q_t, do_t, e_all, m_pair, m_run, l_run, o_t, dq_t, delta, inv, starts,
    g_sum, s_buf, p_buf, ds_buf, bias, o_stage, dq_stage, g_out, g_relay, g_far, g_near, gk_buf, gv_buf,
    local_sem, kv_send, kv_recv, act_send, act_recv, out_send, out_recv, g_send, g_recv,
):
    me = lax.axis_index("ctx")
    core = lax.rem(me, 2)
    other = 1 - core
    chip = me // 2
    partner = me + 1 - 2 * core

    def device(step, which):
        return lax.rem(2 * chip + 2 * step + count, count) + which

    def head_cols(which):
        return pl.ds(pl.multiple_of(which * HEAD, HEAD), HEAD)

    def span_cols(which):
        return pl.ds(pl.multiple_of(which * SPAN, HEAD), SPAN)

    def piece(n):
        return n // 2, pl.ds((n % 2) * PIECE_ROWS, PIECE_ROWS)

    local = [
        pltpu.make_async_copy(q_ref.at[:, span_cols(core)], q_nat.at[core], local_sem.at[0]),
        pltpu.make_async_copy(do_ref.at[:, span_cols(core)], do_nat.at[core], local_sem.at[1]),
        pltpu.make_async_copy(k_ref.at[:, head_cols(core)], kv.at[core, 0], local_sem.at[2]),
        pltpu.make_async_copy(v_ref.at[:, head_cols(core)], kv.at[core, 1], local_sem.at[3]),
    ]
    for copy in local:
        copy.start()
    barrier = pltpu.get_barrier_semaphore()
    for target in (partner, device(-1, 0), device(-1, 1), device(1, 0), device(1, 1)):
        pl.semaphore_signal(barrier, inc=1, device_id={"ctx": target}, device_id_type=MESH)

    m_run[...] = jnp.full_like(m_run, NEGATIVE_FILL)
    l_run[...] = jnp.zeros_like(l_run)
    o_t[...] = jnp.zeros_like(o_t)
    dq_t[...] = jnp.zeros_like(dq_t)
    g_sum[...] = jnp.zeros_like(g_sum)
    for qs in range(2):
        q_pos = (2 * chip + qs) * ROWS + lax.broadcasted_iota(jnp.int32, (8, ROWS), 1)
        start = jnp.zeros((8, ROWS), jnp.int32)
        total = jnp.int32(0)
        for d in range(DOCS):
            total = total + len_ref[d]
            start = jnp.where(q_pos >= total, total, start)
        starts[qs] = start

    def turn_queries(qs):
        for h in range(GROUP):
            cols = slice(h * HEAD, (h + 1) * HEAD)
            q_t[qs, h] = q_nat[qs, :, cols].T
            do_t[qs, h] = do_nat[qs, :, cols].T

    def turn_keys(slot):
        kv_t[slot, 0] = kv[slot, 0].T
        kv_t[slot, 1] = kv[slot, 1].T

    def block_of(slot):
        return 2 * chip + jnp.where(slot < 2, slot, jnp.where(slot == 4, -3, slot - 4))

    def staged(stages, lives):
        for step in range(GROUP + len(stages) - 1):
            for lag, stage in enumerate(stages):
                if 0 <= step - lag < GROUP:
                    stage(step - lag, lives[step - lag])

    def forward(qs, slot, pair):
        q_pos = (2 * chip + qs) * ROWS + lax.broadcasted_iota(jnp.int32, (1, ROWS), 1)
        k_pos = block_of(slot) * ROWS + lax.broadcasted_iota(jnp.int32, (ROWS, ROWS), 0)
        inside = (k_pos <= q_pos) & (k_pos >= starts[qs, 0:1])
        bias[...] = jnp.where(inside, 0.0, NEGATIVE_FILL)

        def scores(h, live):
            s = dot_nn(kv[slot, 0], q_t[qs, h]) + bias[...]
            s_buf[h % 3] = s
            old = m_run[qs, h : h + 1]
            top = jnp.maximum(old, jnp.max(s, axis=0, keepdims=True))
            m_run[qs, h : h + 1] = top
            m_pair[pair, h : h + 1] = top
            live["top"] = top
            live["shrink"] = jnp.exp2((old - top) * LOG2E_SCALE)

        def soft(h, live):
            e = jnp.exp2((s_buf[h % 3] - live["top"]) * LOG2E_SCALE)
            l_run[qs, h : h + 1] = l_run[qs, h : h + 1] * live["shrink"] + jnp.sum(
                e, axis=0, keepdims=True
            )
            e_all[pair, :, h * ROWS : (h + 1) * ROWS] = e.astype(BF16)

        def out(h, live):
            e = e_all[pair, :, h * ROWS : (h + 1) * ROWS]
            o_t[qs, h] = o_t[qs, h] * live["shrink"] + dot_nn(kv_t[slot, 1], e)

        staged((scores, soft, out), [dict() for _ in range(GROUP)])

    def finish_forward(qs):
        for h in range(GROUP):
            r = 1.0 / l_run[qs, h : h + 1]
            low = (o_t[qs, h] * r).astype(BF16)
            o_stage[qs, :, h * HEAD : (h + 1) * HEAD] = low.T
            inv[qs, h : h + 1] = r
            delta[qs, h : h + 1] = jnp.sum(
                do_t[qs, h].astype(F32) * low.astype(F32), axis=0, keepdims=True
            )

    def backward(qs, slot, pair):
        def dprob(h, live):
            s_buf[h % 3] = dot_nn(kv[slot, 1], do_t[qs, h])

        def dscore(h, live):
            rows = slice(h * ROWS, (h + 1) * ROWS)
            one = slice(h, h + 1)
            factor = jnp.exp2((m_pair[pair, one] - m_run[qs, one]) * LOG2E_SCALE) * inv[qs, one]
            p = e_all[pair, :, rows].astype(F32) * factor
            p_buf[:, rows] = p.astype(BF16)
            ds_buf[:, rows] = (p * (s_buf[h % 3] - delta[qs, one])).astype(BF16)

        def grad(h, live):
            rows = slice(h * ROWS, (h + 1) * ROWS)
            cols = slice(h * HEAD, (h + 1) * HEAD)
            dq_t[qs, h] += dot_nn(kv_t[slot, 0], ds_buf[:, rows])
            g_sum[slot, 1] += dot_nn(p_buf[:, rows], do_nat[qs, :, cols])
            g_sum[slot, 0] += dot_nn(ds_buf[:, rows], q_nat[qs, :, cols])

        staged((dprob, dscore, grad), [dict() for _ in range(GROUP)])

    def finish_backward(qs):
        for h in range(GROUP):
            dq_stage[qs, :, h * HEAD : (h + 1) * HEAD] = (dq_t[qs, h] * SCALE).astype(BF16).T

    def grad_piece(slot, n):
        c, rows = piece(n)
        return g_sum[slot, c, rows] * (SCALE if c == 0 else 1.0)

    for copy in local:
        copy.wait()
    turn_queries(core)
    turn_keys(core)
    forward(core, core, 4 * core)
    pl.semaphore_wait(barrier, 5)

    own = (k_ref, v_ref)
    sent = []
    for n in range(PIECES):
        c, rows = piece(n)
        for which, (target, slot, head) in enumerate(
            ((device(1, 0), 2 + core, 0), (device(1, 1), 2 + core, 1), (partner, core, other))
        ):
            copy = remote(
                own[c].at[rows, head_cols(head)], kv.at[slot, c, rows],
                kv_send.at[which, n], kv_recv.at[slot, n], target,
            )
            copy.start()
            sent.append(copy)
    acts = []
    for n, (src, dst) in enumerate(((q_ref, q_nat), (do_ref, do_nat))):
        copy = remote(
            src.at[:, span_cols(other)], dst.at[core], act_send.at[n], act_recv.at[n], partner
        )
        copy.start()
        acts.append(copy)

    def arrived(slot, n):
        c, rows = piece(n)
        remote(
            kv.at[slot, c, rows], kv.at[slot, c, rows], kv_send.at[3, n], kv_recv.at[slot, n], partner
        ).wait_recv()

    for n in range(PIECES):
        arrived(other, n)
    for copy in acts:
        copy.wait_recv()
    turn_queries(other)
    turn_keys(other)

    def chip_pairs(t, carry):
        first = t == 0
        forward(jnp.where(first, other, 1), jnp.where(first, other, 0), jnp.where(first, 4 * other, 5))
        return carry

    lax.fori_loop(0, 2, chip_pairs, 0)

    for n in range(PIECES):
        arrived(3, n)
        c, rows = piece(n)
        copy = remote(
            kv.at[3, c, rows], kv.at[4, c, rows],
            kv_send.at[3, n], kv_recv.at[4, n], device(1, 0) + core,
        )
        copy.start()
        sent.append(copy)
    for n in range(PIECES):
        arrived(2, n)
    turn_keys(3)
    turn_keys(2)

    def before_pairs(t, carry):
        qs = lax.rem(t, 2)
        forward(qs, 3 - t // 2, 5 * qs + 1 + t // 2)
        return carry

    lax.fori_loop(0, 4, before_pairs, 0)
    outs = []

    def hand_out(stage, dst, n, qs):
        here = pltpu.make_async_copy(
            stage.at[qs], dst.at[:, span_cols(core)], local_sem.at[n]
        )
        there = remote(
            stage.at[qs], dst.at[:, span_cols(core)], out_send.at[n], out_recv.at[n], partner
        )

        @pl.when(core == qs)
        def _():
            here.start()

        @pl.when(core != qs)
        def _():
            there.start()

        if qs == 0:
            outs.append((here, there))

    def hand_gradient(slot):
        for n in range(PIECES):
            c, rows = piece(n)

            @pl.when(core != slot)
            def _():
                g_out[3, c, rows] = grad_piece(slot, n).astype(BF16)
                remote(
                    g_out.at[3, c, rows], g_near.at[c, rows], g_send.at[3, n], g_recv.at[3, n], partner
                ).start()

    finish_forward(1)
    hand_out(o_stage, o_ref, 0, 1)

    def odd_back(t, carry):
        backward(1, lax.rem(t + 2, 4), 7 - t)
        return carry

    lax.fori_loop(0, 4, odd_back, 0)
    finish_backward(1)
    hand_out(dq_stage, dq_ref, 1, 1)
    hand_gradient(1)

    for n in range(PIECES):
        arrived(4, n)
    turn_keys(4)
    forward(0, 4, 3)
    finish_forward(0)
    hand_out(o_stage, o_ref, 0, 0)

    def send_gradient(slot, which, n, dst, recv, target):
        c, rows = piece(n)
        remote(
            g_out.at[which, c, rows], dst.at[c, rows], g_send.at[which, n], recv, target
        ).start()

    def even_back(t, carry):
        slot = jnp.where(t == 0, 4, jnp.where(t == 3, 0, 4 - t))
        pair = jnp.where(t == 0, 3, jnp.where(t == 3, 0, t))
        backward(0, slot, pair)

        @pl.when(t == 0)
        def _():
            for n in range(PIECES):
                c, rows = piece(n)
                g_out[0, c, rows] = grad_piece(4, n).astype(BF16)
                send_gradient(4, 0, n, g_relay, g_recv.at[0, n], device(-1, 0) + core)

        @pl.when(t == 2)
        def _():
            for n in range(PIECES):
                c, rows = piece(n)
                g_out[1, c, rows] = grad_piece(2, n).astype(BF16)
                send_gradient(2, 1, n, g_far.at[core], g_recv.at[1 + core, n], device(-1, 0))

        return carry

    lax.fori_loop(0, 4, even_back, 0)
    hand_gradient(0)
    finish_backward(0)
    hand_out(dq_stage, dq_ref, 1, 0)

    for n in range(PIECES):
        c, rows = piece(n)
        remote(
            g_out.at[0, c, rows], g_relay.at[c, rows], g_send.at[0, n], g_recv.at[0, n], partner
        ).wait_recv()
        g_out[2, c, rows] = (grad_piece(3, n) + g_relay[c, rows].astype(F32)).astype(BF16)
        send_gradient(3, 2, n, g_far.at[core], g_recv.at[1 + core, n], device(-1, 1))

    for n in range(PIECES):
        c, rows = piece(n)
        remote(
            g_out.at[3, c, rows], g_near.at[c, rows], g_send.at[3, n], g_recv.at[3, n], partner
        ).wait_recv()
        for head in range(2):
            remote(
                g_out.at[1, c, rows], g_far.at[head, c, rows],
                g_send.at[1, n], g_recv.at[1 + head, n], partner,
            ).wait_recv()
        buf = (gk_buf, gv_buf)[c]
        mine = grad_piece(core, n) + g_far[core, c, rows].astype(F32)
        theirs = g_near[c, rows].astype(F32) + g_far[other, c, rows].astype(F32)
        buf[rows, head_cols(core)] = mine.astype(BF16)
        buf[rows, head_cols(other)] = theirs.astype(BF16)
    ends = [
        pltpu.make_async_copy(gk_buf, gk_ref, local_sem.at[2]),
        pltpu.make_async_copy(gv_buf, gv_ref, local_sem.at[3]),
    ]
    for copy in ends:
        copy.start()
    for copy in ends:
        copy.wait()
    for here, there in outs:
        here.wait()
        there.wait()
    for copy in sent + acts:
        copy.wait_send()
    for which in range(4):
        for n in range(PIECES):
            c, rows = piece(n)
            remote(
                g_out.at[which, c, rows], g_relay.at[c, rows],
                g_send.at[which, n], g_recv.at[0, n], partner,
            ).wait_send()


def per_device(queries, keys, values, output_gradient, lengths):
    count = lax.axis_size("ctx")
    width = KEY_VALUE_HEADS * HEAD
    wide = QUERY_HEADS * HEAD
    dma = pltpu.SemaphoreType.DMA
    vmem = pltpu.VMEM
    shapes = [
        jax.ShapeDtypeStruct((ROWS, wide), BF16),
        jax.ShapeDtypeStruct((ROWS, wide), BF16),
        jax.ShapeDtypeStruct((ROWS, width), BF16),
        jax.ShapeDtypeStruct((ROWS, width), BF16),
    ]
    return pl.pallas_call(
        functools.partial(fused_kernel, count),
        out_shape=shapes,
        in_specs=[SMEM] + [HBM] * 4,
        out_specs=[HBM] * 4,
        scratch_shapes=[
            vmem((SLOTS, 2, ROWS, HEAD), BF16),
            vmem((SLOTS, 2, HEAD, ROWS), BF16),
            vmem((2, ROWS, SPAN), BF16),
            vmem((2, ROWS, SPAN), BF16),
            vmem((2, GROUP, HEAD, ROWS), BF16),
            vmem((2, GROUP, HEAD, ROWS), BF16),
            vmem((8, ROWS, GROUP * ROWS), BF16),
            vmem((8, 8, ROWS), F32),
            vmem((2, 8, ROWS), F32),
            vmem((2, 8, ROWS), F32),
            vmem((2, GROUP, HEAD, ROWS), F32),
            vmem((2, GROUP, HEAD, ROWS), F32),
            vmem((2, 8, ROWS), F32),
            vmem((2, 8, ROWS), F32),
            vmem((2, 8, ROWS), jnp.int32),
            vmem((SLOTS, 2, ROWS, HEAD), F32),
            vmem((3, ROWS, ROWS), F32),
            vmem((ROWS, GROUP * ROWS), BF16),
            vmem((ROWS, GROUP * ROWS), BF16),
            vmem((ROWS, ROWS), F32),
            vmem((2, ROWS, SPAN), BF16),
            vmem((2, ROWS, SPAN), BF16),
            vmem((4, 2, ROWS, HEAD), BF16),
            vmem((2, ROWS, HEAD), BF16),
            vmem((2, 2, ROWS, HEAD), BF16),
            vmem((2, ROWS, HEAD), BF16),
            vmem((ROWS, width), BF16),
            vmem((ROWS, width), BF16),
            dma((4,)),
            dma((4, PIECES)),
            dma((SLOTS, PIECES)),
            dma((2,)),
            dma((2,)),
            dma((2,)),
            dma((2,)),
            dma((4, PIECES)),
            dma((4, PIECES)),
        ],
        compiler_params=pltpu.CompilerParams(
            collective_id=0, has_side_effects=True, vmem_limit_bytes=64 << 20
        ),
        name="attention",
    )(lengths, queries, keys, values, output_gradient)


def solution(mesh):
    split = P(("dp", "ctx"), None)
    return jax.shard_map(
        per_device,
        mesh=mesh,
        in_specs=(split, split, split, split, P("dp")),
        out_specs=(split, split, split, split),
        check_vma=False,
    )
```

time: 93.1 us -> 46.2 us (0.50)
  the two profiles are of different devices: /device:TPU:237 before, /device:TPU:1 now
where the time goes in v2:
time: 46.2 us; the launch traced here: 46 us
  Pallas kernels  40.5 us (88%)
  local copies, waits for them, and re-layouts  4.87 us (11%)
  between operations  0.65 us (1%)
    pallas_call x1, Pallas kernels, per_device(): pl.pallas_call(functools.partial(fused_kernel, count), out_shape=shapes,...  40.5 us
    unnamed x10, local copies, waits for them, and re-layouts  4.87 us

profile of v2, /device:TPU:1, one launch (start us, length us, event | category | flops | bytes accessed | tf_op | source)
XLA Modules:
  0.0 46.0 jit_solution(3014917753157788040)
XLA Ops:
  0.6 40.5 %attention.1 = (bf16[256,1792]{1,0:T(8,128)(2,1)}, bf16[256,1792]{1,0:T(8,128)(2,1)}, bf16[256,256]{1,0:T(8,128)(2,1)}, bf16[256,256]{1,0:T(8,128)(2,1)}) custom-call(s32[32]{0:T(128)} %len_ref.1, bf16[256,1792]{1,0:T(8,128)(2,1)} %q_ref.1, bf16[256,256]{1,0:T(8,128)(2,1)} %k_ref.1, bf16[256,256]{1,0:T(8,128)(2,1)} %v_ref.1, bf16[256,1792]{1,0:T(8,128)(2,1)} %do_ref.1), custom_call_target="tpu_custom_call" | custom-call | tf_op jit(solution)/shard_map/attention/pallas_call | solution.py:388
  41.1 0.0 copy-start
  41.1 2.2 %copy.13 = bf16[256,1792]{1,0:T(8,128)(2,1)} copy(bf16[256,1792]{1,0:T(8,128)(2,1)} %get-tuple-element.8) | data formatting | bytes 1835008
  43.4 0.0 copy-done
  43.4 0.0 copy-start.2
  43.4 0.9 %copy.14 = bf16[256,1792]{1,0:T(8,128)(2,1)} copy(bf16[256,1792]{1,0:T(8,128)(2,1)S(1)} %copy-done) | data formatting | bytes 1835008
  44.3 0.1 copy-done.2
  44.4 0.0 copy-start.1
  44.4 0.7 %copy.15 = bf16[256,256]{1,0:T(8,128)(2,1)} copy(bf16[256,256]{1,0:T(8,128)(2,1)S(1)} %copy-done.2) | data formatting | bytes 262144
  45.1 0.3 copy-done.1
  45.4 0.7 %copy.16 = bf16[256,256]{1,0:T(8,128)(2,1)} copy(bf16[256,256]{1,0:T(8,128)(2,1)S(1)} %copy-done.1) | data formatting | bytes 262144
Async XLA Ops:
  41.1 2.3 %copy-start = (bf16[256,1792]{1,0:T(8,128)(2,1)S(1)}, bf16[256,1792]{1,0:T(8,128)(2,1)}, u32[]{:S(2)}) copy-start(bf16[256,1792]{1,0:T(8,128)(2,1)} %get-tuple-element.9) | copy-start | bytes 2752516
  43.4 1.0 %copy-start.2 = (bf16[256,256]{1,0:T(8,128)(2,1)S(1)}, bf16[256,256]{1,0:T(8,128)(2,1)}, u32[]{:S(2)}) copy-start(bf16[256,256]{1,0:T(8,128)(2,1)} %get-tuple-element.10) | copy-start | bytes 393220
  44.4 1.0 %copy-start.1 = (bf16[256,256]{1,0:T(8,128)(2,1)S(1)}, bf16[256,256]{1,0:T(8,128)(2,1)}, u32[]{:S(2)}) copy-start(bf16[256,256]{1,0:T(8,128)(2,1)} %get-tuple-element.11) | copy-start | bytes 393220

commit v3 on v2

v3 whole, which is shorter than its diff:
```python
import functools
import math

import jax
import jax.numpy as jnp
from jax import lax
from jax.experimental import pallas as pl
from jax.experimental.pallas import tpu as pltpu
from jax.sharding import PartitionSpec as P

QUERY_HEADS = 14
KEY_VALUE_HEADS = 2
HEAD = 128
GROUP = QUERY_HEADS // KEY_VALUE_HEADS
SPAN = GROUP * HEAD
DOCS = 32
ROWS = 256
SLOTS = 5
LANES = GROUP * ROWS
EXTRA = 16
PIECES = 4
PIECE_ROWS = ROWS // 2
NEGATIVE_FILL = -1e30
SCALE = 1.0 / math.sqrt(HEAD)
LOG2E_SCALE = math.log2(math.e) * SCALE
BF16 = jnp.bfloat16
F32 = jnp.float32
MESH = pl.DeviceIdType.MESH
SMEM = pl.BlockSpec(memory_space=pltpu.SMEM)
HBM = pl.BlockSpec(memory_space=pltpu.HBM)
ANY = pl.BlockSpec(memory_space=pl.ANY)


def dot_nn(a, b):
    return lax.dot_general(a, b, (((1,), (0,)), ((), ())), preferred_element_type=F32)


def remote(src, dst, send, recv, target):
    return pltpu.make_async_remote_copy(
        src_ref=src, dst_ref=dst, send_sem=send, recv_sem=recv,
        device_id={"ctx": target}, device_id_type=MESH,
    )


def fused_kernel(
    count, len_ref, q_ref, k_ref, v_ref, do_ref,
    o_ref, dq_ref, gk_ref, gv_ref,
    kv, k_t, v_t, q_nat, do_nat, q_t, do_t, e_all, m_pair, shrink_buf, m_run, o_t, dq_t, delta, inv, starts,
    g_sum, s_buf, p_buf, ds_buf, bias, o_stage, dq_stage, g_out, g_relay, g_far, g_end,
    local_sem, end_sem, kv_send, kv_recv, act_local, act_send, act_recv, out_send, out_recv, g_send, g_recv,
):
    me = lax.axis_index("ctx")
    core = lax.rem(me, 2)
    other = 1 - core
    chip = me // 2
    partner = me + 1 - 2 * core

    ahead = lax.rem(me + 2, count)
    behind = lax.rem(me - 2 + count, count)

    def head_cols(which):
        return pl.ds(pl.multiple_of(which * HEAD, HEAD), HEAD)

    def span_cols(which):
        return pl.ds(pl.multiple_of(which * SPAN, HEAD), SPAN)

    def piece(n):
        return n // 2, pl.ds((n % 2) * PIECE_ROWS, PIECE_ROWS)

    def group_cols(which, h):
        return pl.ds(pl.multiple_of(which * SPAN + h * HEAD, HEAD), HEAD)

    def head_rows(h):
        return pl.ds(h * ROWS, ROWS)

    local = [
        pltpu.make_async_copy(k_ref.at[:, head_cols(core)], kv.at[core, 0], local_sem.at[2]),
        pltpu.make_async_copy(v_ref.at[:, head_cols(core)], kv.at[core, 1], local_sem.at[3]),
    ]
    for n, (src, dst) in enumerate(((q_ref, q_nat), (do_ref, do_nat))):
        for h in range(GROUP):
            local.append(
                pltpu.make_async_copy(
                    src.at[:, group_cols(core, h)], dst.at[core, head_rows(h)], act_local.at[n, h]
                )
            )
    for copy in local:
        copy.start()
    barrier = pltpu.get_barrier_semaphore()
    for target in (partner, ahead, behind):
        pl.semaphore_signal(barrier, inc=1, device_id={"ctx": target}, device_id_type=MESH)

    m_run[...] = jnp.full_like(m_run, NEGATIVE_FILL)
    o_t[...] = jnp.zeros_like(o_t)
    dq_t[...] = jnp.zeros_like(dq_t)
    g_sum[...] = jnp.zeros_like(g_sum)
    for qs in range(2):
        q_pos = (2 * chip + qs) * ROWS + lax.broadcasted_iota(jnp.int32, (8, ROWS), 1)
        start = jnp.zeros((8, ROWS), jnp.int32)
        total = jnp.int32(0)
        for d in range(DOCS):
            total = total + len_ref[d]
            start = jnp.where(q_pos >= total, total, start)
        starts[qs] = start

    def turn_queries(qs):
        for h in range(GROUP):
            lanes = slice(h * ROWS, (h + 1) * ROWS)
            q_t[qs, :, lanes] = q_nat[qs, h * ROWS : (h + 1) * ROWS].T
            do_t[qs, :, lanes] = do_nat[qs, h * ROWS : (h + 1) * ROWS].T

    def turn_keys(slot):
        k_t[slot] = kv[slot, 0].T
        v_t[slot, :HEAD] = kv[slot, 1].T
        v_t[slot, HEAD:] = jnp.ones((EXTRA, ROWS), BF16)

    def block_of(slot):
        return 2 * chip + jnp.where(slot < 2, slot, jnp.where(slot == 4, -3, slot - 4))

    def staged(stages, units):
        for step in range(len(units) + len(stages) - 1):
            for lag, stage in enumerate(stages):
                if 0 <= step - lag < len(units):
                    stage(step - lag, *units[step - lag])

    heads = [slice(h * ROWS, (h + 1) * ROWS) for h in range(GROUP)]

    def forward(units):

        def scores(place, qs, slot, pair):
            q_pos = (2 * chip + qs) * ROWS + lax.broadcasted_iota(jnp.int32, (1, ROWS), 1)
            k_pos = block_of(slot) * ROWS + lax.broadcasted_iota(jnp.int32, (ROWS, ROWS), 0)
            inside = (k_pos <= q_pos) & (k_pos >= starts[qs, 0:1])
            bias[place % 2] = jnp.where(inside, 0.0, NEGATIVE_FILL)
            s = dot_nn(kv[slot, 0], q_t[qs])
            for lanes in heads:
                masked = s[:, lanes] + bias[place % 2]
                s_buf[place % 2, :, lanes] = masked
                old = m_run[qs, 0:1, lanes]
                top = jnp.maximum(old, jnp.max(masked, axis=0, keepdims=True))
                m_run[qs, 0:1, lanes] = top
                m_pair[pair, 0:1, lanes] = top
                shrink_buf[place % 3, 0:1, lanes] = jnp.exp2((old - top) * LOG2E_SCALE)

        def soft(place, qs, slot, pair):
            for lanes in heads:
                top = m_pair[pair, 0:1, lanes]
                e = jnp.exp2((s_buf[place % 2, :, lanes] - top) * LOG2E_SCALE)
                e_all[pair, :, lanes] = e.astype(BF16)

        def out(place, qs, slot, pair):
            o_t[qs] = o_t[qs] * shrink_buf[place % 3, 0:1] + dot_nn(v_t[slot], e_all[pair])

        staged((scores, soft, out), units)

    def finish_forward(qs):
        for h, lanes in enumerate(heads):
            r = 1.0 / o_t[qs, HEAD : HEAD + 1, lanes]
            low = (o_t[qs, :HEAD, lanes] * r).astype(BF16)
            o_stage[qs, :, h * HEAD : (h + 1) * HEAD] = low.T
            inv[qs, 0:1, lanes] = r
            delta[qs, 0:1, lanes] = jnp.sum(
                do_t[qs, :, lanes].astype(F32) * low.astype(F32), axis=0, keepdims=True
            )

    def backward(units):
        def dprob(place, qs, slot, pair):
            s_buf[place % 2] = dot_nn(kv[slot, 1], do_t[qs])

        def dscore(place, qs, slot, pair):
            for lanes in heads:
                factor = jnp.exp2((m_pair[pair, 0:1, lanes] - m_run[qs, 0:1, lanes]) * LOG2E_SCALE)
                factor = factor * inv[qs, 0:1, lanes]
                p = e_all[pair, :, lanes].astype(F32) * factor
                p_buf[place % 2, :, lanes] = p.astype(BF16)
                ds_buf[place % 2, :, lanes] = (p * (s_buf[place % 2, :, lanes] - delta[qs, 0:1, lanes])).astype(
                    BF16
                )

        def grad(place, qs, slot, pair):
            g_sum[slot, 1] += dot_nn(p_buf[place % 2], do_nat[qs])
            g_sum[slot, 0] += dot_nn(ds_buf[place % 2], q_nat[qs])
            dq_t[qs] += dot_nn(k_t[slot], ds_buf[place % 2])

        staged((dprob, dscore, grad), units)

    def finish_backward(qs):
        for h, lanes in enumerate(heads):
            dq_stage[qs, :, h * HEAD : (h + 1) * HEAD] = (dq_t[qs, :, lanes] * SCALE).astype(BF16).T

    def grad_piece(slot, n):
        c, rows = piece(n)
        return g_sum[slot, c, rows] * (SCALE if c == 0 else 1.0)

    for copy in local:
        copy.wait()
    turn_queries(core)
    turn_keys(core)
    forward([(core, core, 4 * core)])
    pl.semaphore_wait(barrier, 3)

    own = (k_ref, v_ref)
    sent = []

    def send_kv(src, dst_slot, which, n, target):
        c, rows = piece(n)
        copy = remote(
            src, kv.at[dst_slot, c, rows], kv_send.at[which, n], kv_recv.at[dst_slot, n], target
        )
        copy.start()
        sent.append(copy)

    for n in range(PIECES):
        c, rows = piece(n)
        send_kv(kv.at[core, c, rows], 2 + core, 0, n, ahead)
    for n in range(PIECES):
        c, rows = piece(n)
        send_kv(own[c].at[rows, head_cols(other)], core, 1, n, partner)
    acts = []
    for n, (src, dst) in enumerate(((q_ref, q_nat), (do_ref, do_nat))):
        for h in range(GROUP):
            copy = remote(
                src.at[:, group_cols(other, h)], dst.at[core, head_rows(h)],
                act_send.at[n, h], act_recv.at[n, h], partner,
            )
            copy.start()
            acts.append(copy)

    def arrived(slot, n):
        c, rows = piece(n)
        remote(
            kv.at[slot, c, rows], kv.at[slot, c, rows], kv_send.at[3, n], kv_recv.at[slot, n], partner
        ).wait_recv()

    for n in range(PIECES):
        arrived(other, n)
        c, rows = piece(n)
        send_kv(kv.at[other, c, rows], 2 + other, 2, n, ahead)
    for copy in acts:
        copy.wait_recv()
    turn_queries(other)
    turn_keys(other)

    forward([(other, other, 4 * other), (1, 0, 5)])

    for n in range(PIECES):
        arrived(3, n)
        c, rows = piece(n)
        send_kv(kv.at[3, c, rows], 4, 3, n, ahead)
    for n in range(PIECES):
        arrived(2, n)
    turn_keys(3)
    turn_keys(2)

    forward([(1, 3, 6), (1, 2, 7), (0, 3, 1), (0, 2, 2)])
    outs = []

    def hand_out(stage, dst, n, qs):
        here = pltpu.make_async_copy(
            stage.at[qs], dst.at[:, span_cols(core)], local_sem.at[n]
        )
        there = remote(
            stage.at[qs], dst.at[:, span_cols(core)], out_send.at[n], out_recv.at[n], partner
        )

        @pl.when(core == qs)
        def _():
            here.start()

        @pl.when(core != qs)
        def _():
            there.start()

        if qs == 0:
            outs.append((here, there))

    def send_gradient(slot, which, dst, extra=None):
        for n in range(PIECES):
            c, rows = piece(n)
            value = grad_piece(slot, n)
            if extra is not None:
                remote(
                    g_out.at[0, c, rows], extra.at[c, rows], g_send.at[0, n], g_recv.at[0, n], partner
                ).wait_recv()
                value = value + extra[c, rows].astype(F32)
            g_out[which, c, rows] = value.astype(BF16)
            remote(
                g_out.at[which, c, rows], dst.at[c, rows],
                g_send.at[which, n], g_recv.at[which, n], behind,
            ).start()

    finish_forward(1)
    hand_out(o_stage, o_ref, 0, 1)
    backward([(1, 2, 7)])

    for n in range(PIECES):
        arrived(4, n)
    turn_keys(4)
    forward([(0, 4, 3)])
    finish_forward(0)
    hand_out(o_stage, o_ref, 0, 0)
    backward([(0, 4, 3)])
    send_gradient(4, 0, g_relay)
    backward([(0, 2, 2)])
    send_gradient(2, 1, g_far.at[0])
    backward([(1, 3, 6), (0, 3, 1), (1, 0, 5)])
    send_gradient(3, 2, g_far.at[1], g_relay)
    backward([(1, 1, 4), (0, 0, 0)])
    finish_backward(1)
    hand_out(dq_stage, dq_ref, 1, 1)
    finish_backward(0)
    hand_out(dq_stage, dq_ref, 1, 0)

    grads = (gk_ref, gv_ref)
    ends = []
    for slot in range(2):
        for n in range(PIECES):
            c, rows = piece(n)
            remote(
                g_out.at[1 + slot, c, rows], g_far.at[slot, c, rows],
                g_send.at[1 + slot, n], g_recv.at[1 + slot, n], partner,
            ).wait_recv()
            g_end[slot, c, rows] = (grad_piece(slot, n) + g_far[slot, c, rows].astype(F32)).astype(
                BF16
            )
            dst = grads[c].at[rows, head_cols(core)]
            here = pltpu.make_async_copy(g_end.at[slot, c, rows], dst, end_sem.at[n])
            there = remote(
                g_end.at[slot, c, rows], dst, g_send.at[3, n], g_recv.at[3, n], partner
            )

            @pl.when(core == slot)
            def _():
                here.start()

            @pl.when(core != slot)
            def _():
                there.start()

            if slot == 1:
                ends.append((here, there))
    for here, there in outs + ends:
        here.wait()
        there.wait()
    for copy in sent + acts:
        copy.wait_send()
    for which in range(3):
        for n in range(PIECES):
            c, rows = piece(n)
            remote(
                g_out.at[which, c, rows], g_relay.at[c, rows],
                g_send.at[which, n], g_recv.at[0, n], partner,
            ).wait_send()


def copy_kernel(*refs):
    half = len(refs) // 2
    copies = [
        pltpu.make_async_copy(refs[n], refs[half + n], refs[-1].at[n]) for n in range(half)
    ]
    for copy in copies:
        copy.start()
    for copy in copies:
        copy.wait()


def per_device(queries, keys, values, output_gradient, lengths):
    count = lax.axis_size("ctx")
    width = KEY_VALUE_HEADS * HEAD
    wide = QUERY_HEADS * HEAD
    operands = (lengths, queries, keys, values, output_gradient)
    dma = pltpu.SemaphoreType.DMA
    vmem = pltpu.VMEM
    shapes = [
        jax.ShapeDtypeStruct((ROWS, wide), BF16),
        jax.ShapeDtypeStruct((ROWS, wide), BF16),
        jax.ShapeDtypeStruct((ROWS, width), BF16),
        jax.ShapeDtypeStruct((ROWS, width), BF16),
    ]
    results = pl.pallas_call(
        functools.partial(fused_kernel, count),
        out_shape=shapes,
        in_specs=[SMEM] + [HBM] * 4,
        out_specs=[ANY] * 4,
        scratch_shapes=[
            vmem((SLOTS, 2, ROWS, HEAD), BF16),
            vmem((SLOTS, HEAD, ROWS), BF16),
            vmem((SLOTS, HEAD + EXTRA, ROWS), BF16),
            vmem((2, LANES, HEAD), BF16),
            vmem((2, LANES, HEAD), BF16),
            vmem((2, HEAD, LANES), BF16),
            vmem((2, HEAD, LANES), BF16),
            vmem((8, ROWS, LANES), BF16),
            vmem((8, 8, LANES), F32),
            vmem((3, 8, LANES), F32),
            vmem((2, 8, LANES), F32),
            vmem((2, HEAD + EXTRA, LANES), F32),
            vmem((2, HEAD, LANES), F32),
            vmem((2, 8, LANES), F32),
            vmem((2, 8, LANES), F32),
            vmem((2, 8, ROWS), jnp.int32),
            vmem((SLOTS, 2, ROWS, HEAD), F32),
            vmem((2, ROWS, LANES), F32),
            vmem((2, ROWS, LANES), BF16),
            vmem((2, ROWS, LANES), BF16),
            vmem((2, ROWS, ROWS), F32),
            vmem((2, ROWS, SPAN), BF16),
            vmem((2, ROWS, SPAN), BF16),
            vmem((3, 2, ROWS, HEAD), BF16),
            vmem((2, ROWS, HEAD), BF16),
            vmem((2, 2, ROWS, HEAD), BF16),
            vmem((2, 2, ROWS, HEAD), BF16),
            dma((4,)),
            dma((PIECES,)),
            dma((4, PIECES)),
            dma((SLOTS, PIECES)),
            dma((2, GROUP)),
            dma((2, GROUP)),
            dma((2, GROUP)),
            dma((2,)),
            dma((2,)),
            dma((4, PIECES)),
            dma((4, PIECES)),
        ],
        compiler_params=pltpu.CompilerParams(
            collective_id=0, has_side_effects=True, vmem_limit_bytes=48 << 20
        ),
        name="attention",
    )(*(pltpu.with_memory_space_constraint(x, pltpu.HBM) for x in operands))
    return pl.pallas_call(
        copy_kernel,
        out_shape=[pltpu.HBM(x.shape, x.dtype) for x in shapes],
        in_specs=[ANY] * 4,
        out_specs=[HBM] * 4,
        scratch_shapes=[dma((4,))],
        name="place_results",
    )(*(pltpu.with_memory_space_constraint(x, pltpu.VMEM) for x in results))


def solution(mesh):
    split = P(("dp", "ctx"), None)
    return jax.shard_map(
        per_device,
        mesh=mesh,
        in_specs=(split, split, split, split, P("dp")),
        out_specs=(split, split, split, split),
        check_vma=False,
    )
```

time: 46.2 us -> 37.2 us (0.81)
  local copies, waits for them, and re-layouts: 4.87 us -> 0 us
  Pallas kernels: 40.5 us -> 36.2 us
    pallas_call x1, Pallas kernels: 40.5 us -> 34.9 us  [per_device(): pl.pallas_call(functools.partial(fused_kernel, count), out_shape=shapes,...]
    unnamed x10 -> x0, local copies, waits for them, and re-layouts: 4.87 us -> none
    pallas_call x0 -> x1, Pallas kernels: none -> 1.34 us  [per_device(): pl.pallas_call(copy_kernel, out_shape=[pltpu.HBM(x.shape, x.dtype) for x...]
where the time goes in v3:
time: 37.2 us; the launch traced here: 37 us
  Pallas kernels  36.2 us (97%)
  between operations  0.8 us (2%)
    pallas_call x1, Pallas kernels, per_device(): pl.pallas_call(functools.partial(fused_kernel, count), out_shape=shapes,...  34.9 us
    pallas_call x1, Pallas kernels, per_device(): pl.pallas_call(copy_kernel, out_shape=[pltpu.HBM(x.shape, x.dtype) for x...  1.34 us

profile of v3, /device:TPU:1, one launch (start us, length us, event | category | flops | bytes accessed | tf_op | source)
XLA Modules:
  0.0 37.0 jit_solution(10430600057071468611)
XLA Ops:
  0.6 34.9 %attention.1 = (bf16[256,1792]{1,0:T(8,128)(2,1)S(1)}, bf16[256,1792]{1,0:T(8,128)(2,1)S(1)}, bf16[256,256]{1,0:T(8,128)(2,1)S(1)}, bf16[256,256]{1,0:T(8,128)(2,1)S(1)}) custom-call(s32[32]{0:T(128)} %len_ref.1, bf16[256,1792]{1,0:T(8,128)(2,1)} %q_ref.1, bf16[256,256]{1,0:T(8,128)(2,1)} %k_ref.1, bf16[256,256]{1,0:T(8,128)(2,1)} %v_ref.1, ...), custom_call_target="tpu_custom_call" | custom-call | tf_op jit(solution)/shard_map/attention/pallas_call | solution.py:380
  35.5 1.3 %place_results.1 = (bf16[256,1792]{1,0:T(8,128)(2,1)}, bf16[256,1792]{1,0:T(8,128)(2,1)}, bf16[256,256]{1,0:T(8,128)(2,1)}, bf16[256,256]{1,0:T(8,128)(2,1)}) custom-call(bf16[256,1792]{1,0:T(8,128)(2,1)S(1)} %get-tuple-element.8.refs_0_, bf16[256,1792]{1,0:T(8,128)(2,1)S(1)} %get-tuple-element.9.refs_1_, bf16[256,256]{1,0:T(8,128)(2,1)S(1)} %get-tuple-element.10.refs_2_, ...), custom_call_target="tpu_custom_call" | custom-call | tf_op jit(solution)/shard_map/place_results/pallas_call | solution.py:430

commit v4 on v3

--- a/solution.py
+++ b/solution.py
@@ -16,10 +16,12 @@
 DOCS = 32
 ROWS = 256
 SLOTS = 5
+RUN = 4
 LANES = GROUP * ROWS
 EXTRA = 16
 PIECES = 4
-PIECE_ROWS = ROWS // 2
+PIECE_ROWS = 2 * ROWS // PIECES
+EARLY = PIECES // 2
 NEGATIVE_FILL = -1e30
 SCALE = 1.0 / math.sqrt(HEAD)
 LOG2E_SCALE = math.log2(math.e) * SCALE
@@ -46,7 +48,7 @@
     count, len_ref, q_ref, k_ref, v_ref, do_ref,
     o_ref, dq_ref, gk_ref, gv_ref,
     kv, k_t, v_t, q_nat, do_nat, q_t, do_t, e_all, m_pair, shrink_buf, m_run, o_t, dq_t, delta, inv, starts,
-    g_sum, s_buf, p_buf, ds_buf, bias, o_stage, dq_stage, g_out, g_relay, g_far, g_end,
+    g_sum, s_buf, p_buf, ds_buf, bias, o_stage, dq_stage, g_out, g_relay, g_direct, g_far, g_end,
     local_sem, end_sem, kv_send, kv_recv, act_local, act_send, act_recv, out_send, out_recv, g_send, g_recv,
 ):
     me = lax.axis_index("ctx")
@@ -65,7 +67,8 @@
         return pl.ds(pl.multiple_of(which * SPAN, HEAD), SPAN)
 
     def piece(n):
-        return n // 2, pl.ds((n % 2) * PIECE_ROWS, PIECE_ROWS)
+        half = PIECES // 2
+        return n // half, pl.ds((n % half) * PIECE_ROWS, PIECE_ROWS)
 
     def group_cols(which, h):
         return pl.ds(pl.multiple_of(which * SPAN + h * HEAD, HEAD), HEAD)
@@ -87,8 +90,51 @@
     for copy in local:
         copy.start()
     barrier = pltpu.get_barrier_semaphore()
-    for target in (partner, ahead, behind):
+    has_next = chip < count // 2 - 1
+    has_prev = chip > 0
+    place_in_run = lax.rem(chip, RUN)
+    far_next = (place_in_run == RUN - 2) & (chip + 2 < count // 2)
+    far_prev = (place_in_run == 0) & (chip >= 2)
+    passes_on = has_next & (place_in_run != RUN - 1)
+    far_ahead = lax.rem(me + 4, count)
+    far_behind = lax.rem(me - 4 + count, count)
+
+    def greet(target):
         pl.semaphore_signal(barrier, inc=1, device_id={"ctx": target}, device_id_type=MESH)
+
+    greet(partner)
+
+    @pl.when(has_next)
+    def _():
+        greet(ahead)
+
+    @pl.when(has_prev)
+    def _():
+        greet(behind)
+
+    @pl.when(far_next)
+    def _():
+        greet(far_ahead)
+
+    @pl.when(far_prev)
+    def _():
+        greet(far_behind)
+
+    @pl.when(chip == 0)
+    def _():
+        kv[2:] = jnp.zeros((SLOTS - 2, 2, ROWS, HEAD), BF16)
+
+    @pl.when(chip == count // 2 - 1)
+    def _():
+        g_far[...] = jnp.zeros_like(g_far)
+
+    @pl.when(jnp.logical_not(passes_on))
+    def _():
+        g_relay[...] = jnp.zeros_like(g_relay)
+
+    @pl.when(jnp.logical_not(far_next))
+    def _():
+        g_direct[...] = jnp.zeros_like(g_direct)
 
     m_run[...] = jnp.full_like(m_run, NEGATIVE_FILL)
     o_t[...] = jnp.zeros_like(o_t)
@@ -109,10 +155,12 @@
             q_t[qs, :, lanes] = q_nat[qs, h * ROWS : (h + 1) * ROWS].T
             do_t[qs, :, lanes] = do_nat[qs, h * ROWS : (h + 1) * ROWS].T
 
-    def turn_keys(slot):
-        k_t[slot] = kv[slot, 0].T
-        v_t[slot, :HEAD] = kv[slot, 1].T
-        v_t[slot, HEAD:] = jnp.ones((EXTRA, ROWS), BF16)
+    def turn_keys(slot, which=(0, 1)):
+        if 0 in which:
+            k_t[slot] = kv[slot, 0].T
+        if 1 in which:
+            v_t[slot, :HEAD] = kv[slot, 1].T
+            v_t[slot, HEAD:] = jnp.ones((EXTRA, ROWS), BF16)
 
     def block_of(slot):
         return 2 * chip + jnp.where(slot < 2, slot, jnp.where(slot == 4, -3, slot - 4))
@@ -125,7 +173,7 @@
 
     heads = [slice(h * ROWS, (h + 1) * ROWS) for h in range(GROUP)]
 
-    def forward(units):
+    def forward(units, before_out=None):
 
         def scores(place, qs, slot, pair):
             q_pos = (2 * chip + qs) * ROWS + lax.broadcasted_iota(jnp.int32, (1, ROWS), 1)
@@ -151,7 +199,12 @@
         def out(place, qs, slot, pair):
             o_t[qs] = o_t[qs] * shrink_buf[place % 3, 0:1] + dot_nn(v_t[slot], e_all[pair])
 
-        staged((scores, soft, out), units)
+        if before_out is None:
+            staged((scores, soft, out), units)
+        else:
+            staged((scores, soft), units)
+            before_out()
+            staged((out,), units)
 
     def finish_forward(qs):
         for h, lanes in enumerate(heads):
@@ -163,7 +216,7 @@
                 do_t[qs, :, lanes].astype(F32) * low.astype(F32), axis=0, keepdims=True
             )
 
-    def backward(units):
+    def backward(units, between=None, after=None):
         def dprob(place, qs, slot, pair):
             s_buf[place % 2] = dot_nn(kv[slot, 1], do_t[qs])
 
@@ -179,7 +232,11 @@
 
         def grad(place, qs, slot, pair):
             g_sum[slot, 1] += dot_nn(p_buf[place % 2], do_nat[qs])
+            if between is not None:
+                between()
             g_sum[slot, 0] += dot_nn(ds_buf[place % 2], q_nat[qs])
+            if after is not None:
+                after()
             dq_t[qs] += dot_nn(k_t[slot], ds_buf[place % 2])
 
         staged((dprob, dscore, grad), units)
@@ -197,7 +254,10 @@
     turn_queries(core)
     turn_keys(core)
     forward([(core, core, 4 * core)])
-    pl.semaphore_wait(barrier, 3)
+    greeted = 1
+    for flag in (has_next, has_prev, far_next, far_prev):
+        greeted = greeted + flag.astype(jnp.int32)
+    pl.semaphore_wait(barrier, greeted)
 
     own = (k_ref, v_ref)
     sent = []
@@ -208,14 +268,27 @@
             src, kv.at[dst_slot, c, rows], kv_send.at[which, n], kv_recv.at[dst_slot, n], target
         )
         copy.start()
-        sent.append(copy)
+        return copy
+
+    def send_own(n):
+        c, rows = piece(n)
+        send_kv(kv.at[core, c, rows], 2 + core, 0, n, ahead)
+
+    def send_other(n):
+        c, rows = piece(n)
+        send_kv(kv.at[other, c, rows], 2 + other, 2, n, ahead)
 
     for n in range(PIECES):
         c, rows = piece(n)
-        send_kv(kv.at[core, c, rows], 2 + core, 0, n, ahead)
+        sent.append(send_kv(own[c].at[rows, head_cols(other)], core, 1, n, partner))
+
+    early = jnp.where(core == 1, PIECES, EARLY)
     for n in range(PIECES):
-        c, rows = piece(n)
-        send_kv(own[c].at[rows, head_cols(other)], core, 1, n, partner)
+
+        @pl.when(has_next & (n < early))
+        def _():
+            send_own(n)
+
     acts = []
     for n, (src, dst) in enumerate(((q_ref, q_nat), (do_ref, do_nat))):
         for h in range(GROUP):
@@ -228,14 +301,38 @@
 
     def arrived(slot, n):
         c, rows = piece(n)
-        remote(
+        copy = remote(
             kv.at[slot, c, rows], kv.at[slot, c, rows], kv_send.at[3, n], kv_recv.at[slot, n], partner
-        ).wait_recv()
+        )
+        if isinstance(slot, int):
+
+            @pl.when(has_prev)
+            def _():
+                copy.wait_recv()
+
+        else:
+            copy.wait_recv()
 
     for n in range(PIECES):
         arrived(other, n)
-        c, rows = piece(n)
-        send_kv(kv.at[other, c, rows], 2 + other, 2, n, ahead)
+
+        @pl.when(has_next)
+        def _():
+            send_other(n)
+
+    for n in range(EARLY, PIECES):
+
+        @pl.when(has_next & (core == 0))
+        def _():
+            send_own(n)
+
+    for n in range(PIECES):
+
+        @pl.when(far_next)
+        def _():
+            c, rows = piece(n)
+            send_kv(kv.at[1, c, rows], 4, 4, n, far_ahead)
+
     for copy in acts:
         copy.wait_recv()
     turn_queries(other)
@@ -245,8 +342,12 @@
 
     for n in range(PIECES):
         arrived(3, n)
-        c, rows = piece(n)
-        send_kv(kv.at[3, c, rows], 4, 3, n, ahead)
+
+        @pl.when(passes_on)
+        def _():
+            c, rows = piece(n)
+            send_kv(kv.at[3, c, rows], 4, 3, n, ahead)
+
     for n in range(PIECES):
         arrived(2, n)
     turn_keys(3)
@@ -274,38 +375,64 @@
         if qs == 0:
             outs.append((here, there))
 
-    def send_gradient(slot, which, dst, extra=None):
-        for n in range(PIECES):
+    def send_gradient(slot, which, dst, extra=None, pieces=range(PIECES)):
+        for n in pieces:
             c, rows = piece(n)
             value = grad_piece(slot, n)
             if extra is not None:
-                remote(
-                    g_out.at[0, c, rows], extra.at[c, rows], g_send.at[0, n], g_recv.at[0, n], partner
-                ).wait_recv()
+
+                @pl.when(passes_on)
+                def _():
+                    remote(
+                        g_out.at[0, c, rows], extra.at[c, rows],
+                        g_send.at[0, n], g_recv.at[0, n], partner,
+                    ).wait_recv()
+
                 value = value + extra[c, rows].astype(F32)
             g_out[which, c, rows] = value.astype(BF16)
-            remote(
-                g_out.at[which, c, rows], dst.at[c, rows],
-                g_send.at[which, n], g_recv.at[which, n], behind,
-            ).start()
+
+            near = has_prev
+            if which == 0:
+                near = has_prev & (place_in_run > 0)
+
+                @pl.when(far_prev)
+                def _():
+                    remote(
+                        g_out.at[which, c, rows], g_direct.at[c, rows],
+                        g_send.at[which, n], g_recv.at[4, n], far_behind,
+                    ).start()
+
+            @pl.when(near)
+            def _():
+                remote(
+                    g_out.at[which, c, rows], dst.at[c, rows],
+                    g_send.at[which, n], g_recv.at[which, n], behind,
+                ).start()
 
     finish_forward(1)
     hand_out(o_stage, o_ref, 0, 1)
-    backward([(1, 2, 7)])
-
-    for n in range(PIECES):
+    for n in range(PIECES // 2):
         arrived(4, n)
-    turn_keys(4)
-    forward([(0, 4, 3)])
+
+    def last_values():
+        for n in range(PIECES // 2, PIECES):
+            arrived(4, n)
+        turn_keys(4)
+
+    forward([(0, 4, 3)], last_values)
     finish_forward(0)
     hand_out(o_stage, o_ref, 0, 0)
-    backward([(0, 4, 3)])
-    send_gradient(4, 0, g_relay)
-    backward([(0, 2, 2)])
+    halves = (range(PIECES // 2), range(PIECES // 2, PIECES))
+    backward(
+        [(0, 4, 3)],
+        lambda: send_gradient(4, 0, g_relay, pieces=halves[1]),
+        lambda: send_gradient(4, 0, g_relay, pieces=halves[0]),
+    )
+    backward([(1, 2, 7), (0, 2, 2)])
     send_gradient(2, 1, g_far.at[0])
-    backward([(1, 3, 6), (0, 3, 1), (1, 0, 5)])
+    backward([(1, 3, 6), (0, 3, 1)])
     send_gradient(3, 2, g_far.at[1], g_relay)
-    backward([(1, 1, 4), (0, 0, 0)])
+    backward([(1, 0, 5), (1, 1, 4), (0, 0, 0)])
     finish_backward(1)
     hand_out(dq_stage, dq_ref, 1, 1)
     finish_backward(0)
@@ -316,13 +443,26 @@
     for slot in range(2):
         for n in range(PIECES):
             c, rows = piece(n)
-            remote(
-                g_out.at[1 + slot, c, rows], g_far.at[slot, c, rows],
-                g_send.at[1 + slot, n], g_recv.at[1 + slot, n], partner,
-            ).wait_recv()
-            g_end[slot, c, rows] = (grad_piece(slot, n) + g_far[slot, c, rows].astype(F32)).astype(
-                BF16
-            )
+
+            @pl.when(has_next)
+            def _():
+                remote(
+                    g_out.at[1 + slot, c, rows], g_far.at[slot, c, rows],
+                    g_send.at[1 + slot, n], g_recv.at[1 + slot, n], partner,
+                ).wait_recv()
+
+            value = grad_piece(slot, n) + g_far[slot, c, rows].astype(F32)
+            if slot == 1:
+
+                @pl.when(far_next)
+                def _():
+                    remote(
+                        g_out.at[0, c, rows], g_direct.at[c, rows],
+                        g_send.at[0, n], g_recv.at[4, n], partner,
+                    ).wait_recv()
+
+                value = value + g_direct[c, rows].astype(F32)
+            g_end[slot, c, rows] = value.astype(BF16)
             dst = grads[c].at[rows, head_cols(core)]
             here = pltpu.make_async_copy(g_end.at[slot, c, rows], dst, end_sem.at[n])
             there = remote(
@@ -344,13 +484,38 @@
         there.wait()
     for copy in sent + acts:
         copy.wait_send()
-    for which in range(3):
-        for n in range(PIECES):
-            c, rows = piece(n)
+    for n in range(PIECES):
+        c, rows = piece(n)
+
+        def gone(which):
+            remote(
+                kv.at[0, c, rows], kv.at[0, c, rows],
+                kv_send.at[which, n], kv_recv.at[0, n], partner,
+            ).wait_send()
+
+        def gone_gradient(which):
             remote(
                 g_out.at[which, c, rows], g_relay.at[c, rows],
                 g_send.at[which, n], g_recv.at[0, n], partner,
             ).wait_send()
+
+        @pl.when(has_next)
+        def _():
+            gone(0)
+            gone(2)
+
+        @pl.when(passes_on)
+        def _():
+            gone(3)
+
+        @pl.when(far_next)
+        def _():
+            gone(4)
+
+        @pl.when(has_prev)
+        def _():
+            for which in range(3):
+                gone_gradient(which)
 
 
 def copy_kernel(*refs):
@@ -408,11 +573,12 @@
             vmem((2, ROWS, SPAN), BF16),
             vmem((3, 2, ROWS, HEAD), BF16),
             vmem((2, ROWS, HEAD), BF16),
+            vmem((2, ROWS, HEAD), BF16),
             vmem((2, 2, ROWS, HEAD), BF16),
             vmem((2, 2, ROWS, HEAD), BF16),
             dma((4,)),
             dma((PIECES,)),
-            dma((4, PIECES)),
+            dma((5, PIECES)),
             dma((SLOTS, PIECES)),
             dma((2, GROUP)),
             dma((2, GROUP)),
@@ -420,7 +586,7 @@
             dma((2,)),
             dma((2,)),
             dma((4, PIECES)),
-            dma((4, PIECES)),
+            dma((5, PIECES)),
         ],
         compiler_params=pltpu.CompilerParams(
             collective_id=0, has_side_effects=True, vmem_limit_bytes=48 << 20

time: 37.2 us -> 33.6 us (0.903)
  the two profiles are of different devices: /device:TPU:1 before, /device:TPU:27 now
where the time goes in v4:
time: 33.6 us; the launch traced here: 33.4 us
  Pallas kernels  32.6 us (97%)
  between operations  0.8 us (2%)
    pallas_call x1, Pallas kernels, per_device(): pl.pallas_call(functools.partial(fused_kernel, count), out_shape=shapes,...  31.3 us
    pallas_call x1, Pallas kernels, per_device(): pl.pallas_call(copy_kernel, out_shape=[pltpu.HBM(x.shape, x.dtype) for x...  1.34 us

profile of v4, /device:TPU:27, one launch (start us, length us, event | category | flops | bytes accessed | tf_op | source)
XLA Modules:
  0.0 33.4 jit_solution(16336655984535646901)
XLA Ops:
  0.6 31.3 %attention.1 = (bf16[256,1792]{1,0:T(8,128)(2,1)S(1)}, bf16[256,1792]{1,0:T(8,128)(2,1)S(1)}, bf16[256,256]{1,0:T(8,128)(2,1)S(1)}, bf16[256,256]{1,0:T(8,128)(2,1)S(1)}) custom-call(s32[32]{0:T(128)} %len_ref.1, bf16[256,1792]{1,0:T(8,128)(2,1)} %q_ref.1, bf16[256,256]{1,0:T(8,128)(2,1)} %k_ref.1, bf16[256,256]{1,0:T(8,128)(2,1)} %v_ref.1, ...), custom_call_target="tpu_custom_call" | custom-call | tf_op jit(solution)/shard_map/attention/pallas_call | solution.py:545
  31.9 1.3 %place_results.1 = (bf16[256,1792]{1,0:T(8,128)(2,1)}, bf16[256,1792]{1,0:T(8,128)(2,1)}, bf16[256,256]{1,0:T(8,128)(2,1)}, bf16[256,256]{1,0:T(8,128)(2,1)}) custom-call(bf16[256,1792]{1,0:T(8,128)(2,1)S(1)} %get-tuple-element.8.refs_0_, bf16[256,1792]{1,0:T(8,128)(2,1)S(1)} %get-tuple-element.9.refs_1_, bf16[256,256]{1,0:T(8,128)(2,1)S(1)} %get-tuple-element.10.refs_2_, ...), custom_call_target="tpu_custom_call" | custom-call | tf_op jit(solution)/shard_map/place_results/pallas_call | solution.py:596

commit v5 on v4

--- a/solution.py
+++ b/solution.py
@@ -348,12 +348,13 @@
             c, rows = piece(n)
             send_kv(kv.at[3, c, rows], 4, 3, n, ahead)
 
+    turn_keys(3)
+    forward([(1, 3, 6), (0, 3, 1)])
     for n in range(PIECES):
         arrived(2, n)
-    turn_keys(3)
     turn_keys(2)
 
-    forward([(1, 3, 6), (1, 2, 7), (0, 3, 1), (0, 2, 2)])
+    forward([(1, 2, 7), (0, 2, 2)])
     outs = []
 
     def hand_out(stage, dst, n, qs):

time: 33.6 us -> 33.3 us (level)
  the two profiles are of different devices: /device:TPU:27 before, /device:TPU:29 now
where the time goes in v5:
time: 33.3 us; the launch traced here: 33.1 us
  Pallas kernels  32.3 us (97%)
  between operations  0.8 us (2%)
    pallas_call x1, Pallas kernels, per_device(): pl.pallas_call(functools.partial(fused_kernel, count), out_shape=shapes,...  31 us
    pallas_call x1, Pallas kernels, per_device(): pl.pallas_call(copy_kernel, out_shape=[pltpu.HBM(x.shape, x.dtype) for x...  1.34 us

profile of v5, /device:TPU:29, one launch (start us, length us, event | category | flops | bytes accessed | tf_op | source)
XLA Modules:
  0.0 33.1 jit_solution(2199950103013856765)
XLA Ops:
  0.6 31.0 %attention.1 = (bf16[256,1792]{1,0:T(8,128)(2,1)S(1)}, bf16[256,1792]{1,0:T(8,128)(2,1)S(1)}, bf16[256,256]{1,0:T(8,128)(2,1)S(1)}, bf16[256,256]{1,0:T(8,128)(2,1)S(1)}) custom-call(s32[32]{0:T(128)} %len_ref.1, bf16[256,1792]{1,0:T(8,128)(2,1)} %q_ref.1, bf16[256,256]{1,0:T(8,128)(2,1)} %k_ref.1, bf16[256,256]{1,0:T(8,128)(2,1)} %v_ref.1, ...), custom_call_target="tpu_custom_call" | custom-call | tf_op jit(solution)/shard_map/attention/pallas_call | solution.py:546
  31.6 1.3 %place_results.1 = (bf16[256,1792]{1,0:T(8,128)(2,1)}, bf16[256,1792]{1,0:T(8,128)(2,1)}, bf16[256,256]{1,0:T(8,128)(2,1)}, bf16[256,256]{1,0:T(8,128)(2,1)}) custom-call(bf16[256,1792]{1,0:T(8,128)(2,1)S(1)} %get-tuple-element.8.refs_0_, bf16[256,1792]{1,0:T(8,128)(2,1)S(1)} %get-tuple-element.9.refs_1_, bf16[256,256]{1,0:T(8,128)(2,1)S(1)} %get-tuple-element.10.refs_2_, ...), custom_call_target="tpu_custom_call" | custom-call | tf_op jit(solution)/shard_map/place_results/pallas_call | solution.py:597
